TPU v7x, 32 devices: a whole 2x2x4 slice. The times are simulated.
32 devices in a mesh: space: 4 (over y, core), ctx: 8 (over z, x).
Axes of the slice: x: 2, y: 2, z: 4, core: 2. Of those that a mesh axis runs over, the one named last changes fastest.
Arguments:
- feats: bfloat16 [4, 8192, 256], P('space', 'ctx'), may hold values from -6 to 6
- face_rows: int32 [4, 2048], P('space', 'ctx'), may hold values from 0 to 1023
- neighbours: int32 [4, 8192, 6], P('space', 'ctx'), may hold values from 0 to 2048
- block_len: int32 [4, 64], P('space'), may hold values from 32 to 128
- dilated: int32 [4, 64, 4], P('space', 'ctx'), may hold values from 0 to 7, as said below
- pick: int32 [4, 8, 8], P('space'), may hold values from 0 to 7
- cpe_weight: bfloat16 [7, 256, 256], replicated, may hold values from -0.125 to 0.125
- cpe_bias: float32 [256], replicated, may hold values from -3 to 3
- ln_gain: float32 [256], replicated, may hold values from 0.1 to 1.9
- ln_bias: float32 [256], replicated, may hold values from -3 to 3
- w_qkv: bfloat16 [256, 768], replicated, may hold values from -11 to 11
- w_out: bfloat16 [256, 256], replicated, may hold values from -3 to 3
Outputs:
- mixed: bfloat16 [4, 8192, 256], P('space', 'ctx')
Inputs may be any that keep to these rules, and one draw needn't show every extreme that they name: `dilated`: among the 32 entries of the blocks of one range, every value 0 to 7 appears.
All inputs are finite; a program needn't handle non-finite values.
Results may differ from a plain program's by a relative error of at most 0.009.
The roundings to bfloat16 on the way count: a program that leaves them out, or rounds other values in their place, can miss the bound.
Values may be sent and summed in bfloat16 or wider, within the bound.
A program may use at most 128 MiB of HBM per device.

v0:
```python
import math

import jax
import jax.numpy as jnp
from jax import lax
from jax.sharding import PartitionSpec as P

D = 256
HEADS = 8
BLK = 128
EDGE = 128
FACE = 256


def extended(block, sides, width):
    for axis, dim in sides:
        count = lax.axis_size(axis)
        forward = [(i, i + 1) for i in range(count - 1)]
        backward = [(target, source) for source, target in forward]
        low = lax.ppermute(
            lax.slice_in_dim(block, block.shape[dim] - width, None, axis=dim), axis, forward
        )
        high = lax.ppermute(lax.slice_in_dim(block, 0, width, axis=dim), axis, backward)
        block = jnp.concatenate([low, block, high], axis=dim)
    return block


def layer_norm(hidden, ln_gain, ln_bias):
    center = hidden - jnp.mean(hidden, axis=-1, keepdims=True)
    variance = jnp.mean(center * center, axis=-1, keepdims=True)
    return (center * lax.rsqrt(variance + 1e-05) * ln_gain + ln_bias).astype(jnp.bfloat16)


def attend(query_blk, key_rows, value_rows, valid_keys):
    rows_q = query_blk.shape[0]
    head_dim = D // HEADS
    query_heads = query_blk.reshape(rows_q, HEADS, head_dim)
    key_heads = key_rows.reshape(-1, HEADS, head_dim)
    value_heads = value_rows.reshape(-1, HEADS, head_dim)
    scores = jnp.einsum(
        "qhd,khd->hqk", query_heads, key_heads, preferred_element_type=jnp.float32
    ) * (1.0 / math.sqrt(head_dim))
    scores = jnp.where(valid_keys[None, None, :], scores, -1e30)
    row_peak = jnp.max(scores, axis=-1, keepdims=True)
    raw_weights = jnp.exp(scores - row_peak)
    denominator = jnp.sum(raw_weights, axis=-1, keepdims=True)
    attn_weights = (raw_weights / denominator).astype(jnp.bfloat16)
    mixed_heads = jnp.einsum(
        "hqk,khd->qhd", attn_weights, value_heads, preferred_element_type=jnp.float32
    )
    return mixed_heads.reshape(rows_q, D).astype(jnp.bfloat16)


def on_device(
    feats,
    face_rows,
    neighbours,
    block_len,
    dilated,
    pick,
    cpe_weight,
    cpe_bias,
    ln_gain,
    ln_bias,
    w_qkv,
    w_out,
):
    voxels = feats[0]
    count_vox = voxels.shape[0]
    feat_width = voxels.shape[1]
    blocks_dev = count_vox // BLK
    my_range = lax.axis_index("ctx")
    edge_rows = extended(voxels, (("ctx", 0),), EDGE)
    face_out = voxels[face_rows[0]]
    face_all = extended(face_out, (("space", 0),), FACE)
    neighbour_table = jnp.concatenate(
        [edge_rows, face_all, jnp.zeros((1, feat_width), voxels.dtype)], 0
    )
    offset_ids = jnp.transpose(neighbours[0])
    conv_out = jnp.dot(voxels, cpe_weight[0], preferred_element_type=jnp.float32)
    for offset in range(6):
        offset_rows = jnp.take(neighbour_table, offset_ids[offset], axis=0)
        conv_out = conv_out + jnp.dot(
            offset_rows, cpe_weight[offset + 1], preferred_element_type=jnp.float32
        )
    hidden = voxels.astype(jnp.float32) + conv_out + cpe_bias
    normed = layer_norm(hidden, ln_gain, ln_bias)
    projected = jnp.dot(normed, w_qkv, preferred_element_type=jnp.float32)
    queries = projected[:, :feat_width].astype(jnp.bfloat16)
    key_value = projected[:, feat_width:].astype(jnp.bfloat16)
    window_kv = extended(key_value, (("ctx", 0),), BLK)
    pick_tile = pick[0]
    send_index = pick_tile[my_range]
    recv_index = pick_tile[:, my_range]
    outgoing = key_value.reshape(blocks_dev, BLK, 2 * feat_width)[send_index]
    remote_kv = lax.all_to_all(outgoing, "ctx", split_axis=0, concat_axis=0, tiled=True)
    lens_tile = block_len[0]
    lens_ext = jnp.pad(lens_tile, (1, 1))
    local_ids = jnp.arange(blocks_dev, dtype=jnp.int32)
    global_ids = my_range * blocks_dev + local_ids
    win_lens = lens_ext[global_ids[:, None] + jnp.arange(3, dtype=jnp.int32)[None, :]]
    slot_ids = dilated[0]
    far_ids = slot_ids * blocks_dev + recv_index[slot_ids]
    far_lens = lens_tile[far_ids]
    key_lens = jnp.concatenate([win_lens, far_lens], 1)
    positions = jnp.arange(BLK, dtype=jnp.int32)

    def one_block(local_id, lens_row, slot_row):
        query_blk = lax.dynamic_slice_in_dim(queries, local_id * BLK, BLK, 0)
        window_rows = lax.dynamic_slice_in_dim(window_kv, local_id * BLK, 3 * BLK, 0)
        remote_rows = remote_kv[slot_row].reshape(-1, 2 * feat_width)
        keys_all = jnp.concatenate([window_rows, remote_rows], 0)
        valid_keys = (positions[None, :] < lens_row[:, None]).reshape(-1)
        return attend(query_blk, keys_all[:, :feat_width], keys_all[:, feat_width:], valid_keys)

    group_size = 4

    def one_group(group_inputs):
        return jax.vmap(one_block)(group_inputs[0], group_inputs[1], group_inputs[2])

    group_inputs = (
        local_ids.reshape(-1, group_size),
        key_lens.reshape(-1, group_size, key_lens.shape[1]),
        slot_ids.reshape(-1, group_size, slot_ids.shape[1]),
    )
    mixed_blocks = lax.map(one_group, group_inputs)
    attended = mixed_blocks.reshape(count_vox, feat_width)
    output = hidden + jnp.dot(attended, w_out, preferred_element_type=jnp.float32)
    return output.astype(jnp.bfloat16)[None]


def solution(mesh):
    placed = (
        P("space", "ctx", None),
        P("space", "ctx"),
        P("space", "ctx", None),
        P("space", None),
        P("space", "ctx", None),
        P("space", None, None),
        P(),
        P(),
        P(),
        P(),
        P(),
        P(),
    )
    return jax.shard_map(
        on_device, mesh=mesh, in_specs=placed, out_specs=P("space", "ctx", None), check_vma=False
    )
```

profile of v0, /device:TPU:16, one launch (start us, length us, event | category | flops | bytes accessed | tf_op | source)
XLA Modules:
  0.0 197.1 jit_solution(857254290216503092)
XLA Ops:
  8.0 3.4 %collective-permute-start = (bf16[128,256]{0,1:T(8,128)(2,1)S(1)}, bf16[128,256]{0,1:T(8,128)(2,1)S(1)}, u32[]{:S(2)}, u32[]{:S(2)}) collective-permute-start(bf16[128,256]{0,1:T(8,128)(2,1)S(1)} %get-tuple-element.147), channel_id=1, source_target_pairs={{0,1},{1,2},{2,3},{3,4},{4,5},{5,6},{6,7},{8,9},{9,10},{10,11},{11... | collective-permute-start | bytes 196616 | tf_op jit(solution)/shard_map/ppermute | solution.py:20
  11.4 3.3 %collective-permute-start.1 = (bf16[128,256]{0,1:T(8,128)(2,1)S(1)}, bf16[128,256]{0,1:T(8,128)(2,1)S(1)}, u32[]{:S(2)}, u32[]{:S(2)}) collective-permute-start(bf16[128,256]{0,1:T(8,128)(2,1)S(1)} %get-tuple-element.146), channel_id=1, source_target_pairs={{1,0},{2,1},{3,2},{4,3},{5,4},{6,5},{7,6},{9,8},{10,9},{11,10},{12... | collective-permute-start | bytes 196616 | tf_op jit(solution)/shard_map/ppermute | solution.py:23
  25.9 5.0 %gather_fusion.6 = bf16[1024,256]{1,0:T(8,128)(2,1)} fusion(bf16[2049,256]{1,0:T(8,128)(2,1)S(1)} %copy.45, s32[1024]{0:T(1024)S(1)} %get-tuple-element.160), kind=kCustom, calls=%fused_computation.clone | custom fusion | bytes 1052672 | tf_op jit(solution)/shard_map/jit(_take)/gather | solution.py:82
  30.9 4.9 %gather_fusion.7 = bf16[1024,256]{1,0:T(8,128)(2,1)} fusion(bf16[2049,256]{1,0:T(8,128)(2,1)S(1)} %copy.45, s32[1024]{0:T(1024)S(1)} %get-tuple-element.161), kind=kCustom, calls=%fused_computation.2.clone | custom fusion | bytes 1052672 | tf_op jit(solution)/shard_map/jit(_take)/gather | solution.py:82
  35.8 4.9 %gather_fusion.8 = bf16[1024,256]{1,0:T(8,128)(2,1)} fusion(bf16[2049,256]{1,0:T(8,128)(2,1)S(1)} %copy.45, s32[1024]{0:T(1024)S(1)} %get-tuple-element.162), kind=kCustom, calls=%fused_computation.3.clone | custom fusion | bytes 1052672 | tf_op jit(solution)/shard_map/jit(_take)/gather | solution.py:82
  40.8 4.9 %gather_fusion.9 = bf16[1024,256]{1,0:T(8,128)(2,1)} fusion(bf16[2049,256]{1,0:T(8,128)(2,1)S(1)} %copy.45, s32[1024]{0:T(1024)S(1)} %get-tuple-element.163), kind=kCustom, calls=%fused_computation.4.clone | custom fusion | bytes 1052672 | tf_op jit(solution)/shard_map/jit(_take)/gather | solution.py:82
  45.7 3.9 %gather_fusion.10 = bf16[1024,256]{1,0:T(8,128)(2,1)S(1)} fusion(bf16[2049,256]{1,0:T(8,128)(2,1)S(1)} %copy.45, s32[1024]{0:T(1024)S(1)} %get-tuple-element.164), kind=kCustom, calls=%fused_computation.5.clone | custom fusion | bytes 1052672 | tf_op jit(solution)/shard_map/jit(_take)/gather | solution.py:82
  49.6 5.0 %gather_fusion.11 = bf16[1024,256]{1,0:T(8,128)(2,1)} fusion(bf16[2049,256]{1,0:T(8,128)(2,1)S(1)} %copy.45, s32[1024]{0:T(1024)S(1)} %get-tuple-element.165), kind=kCustom, calls=%fused_computation.6.clone | custom fusion | bytes 1052672 | tf_op jit(solution)/shard_map/jit(_take)/gather | solution.py:82
  64.7 5.2 %all-to-all-start = ((bf16[8,128,512]{2,1,0:T(8,128)(2,1)}), bf16[8,128,512]{2,1,0:T(8,128)(2,1)S(1)}, u32[]{:S(2)}, u32[]{:S(2)}) async-start(bf16[8,128,512]{2,1,0:T(8,128)(2,1)} %gather_fusion.2), calls=%async_computation | async-start | bytes 2097152 | tf_op jit(solution)/shard_map/all_to_all | solution.py:96
  72.1 3.4 %collective-permute-start.4 = (bf16[128,512]{1,0:T(8,128)(2,1)S(1)}, bf16[128,512]{1,0:T(8,128)(2,1)S(1)}, u32[]{:S(2)}, u32[]{:S(2)}) collective-permute-start(bf16[128,512]{1,0:T(8,128)(2,1)S(1)} %get-tuple-element.144), channel_id=1, source_target_pairs={{0,1},{1,2},{2,3},{3,4},{4,5},{5,6},{6,7},{8,9},{9,10},{10,11},{11... | collective-permute-start | bytes 393224 | tf_op jit(solution)/shard_map/ppermute | solution.py:20
  75.5 3.6 %collective-permute-start.5 = (bf16[128,512]{1,0:T(8,128)(2,1)S(1)}, bf16[128,512]{1,0:T(8,128)(2,1)S(1)}, u32[]{:S(2)}, u32[]{:S(2)}) collective-permute-start(bf16[128,512]{1,0:T(8,128)(2,1)S(1)} %get-tuple-element.145), channel_id=1, source_target_pairs={{1,0},{2,1},{3,2},{4,3},{5,4},{6,5},{7,6},{9,8},{10,9},{11,10},{12... | collective-permute-start | bytes 393224 | tf_op jit(solution)/shard_map/ppermute | solution.py:23
  83.8 14.6 %collective-permute-done.4 = bf16[128,512]{1,0:T(8,128)(2,1)S(1)} collective-permute-done((bf16[128,512]{1,0:T(8,128)(2,1)S(1)}, bf16[128,512]{1,0:T(8,128)(2,1)S(1)}, u32[]{:S(2)}, u32[]{:S(2)}) %collective-permute-start.4) | collective-permute-done | bytes 131104 | tf_op jit(solution)/shard_map/ppermute | solution.py:20
  99.7 94.6 %while.19 = (s32[]{:T(128)}, bf16[2,4,128,256]{3,2,1,0:T(8,128)(2,1)}, s32[2,4]{1,0:T(2,128)}, bf16[1280,512]{1,0:T(8,128)(2,1)S(1)}, s32[2,4,4]{2,1,0:T(4,128)S...) while((s32[]{:T(128)}, ...), condition=%wide.region_5.7_spmd.clone, body=%wide.region_2.6_spmd.clone.sunk | while | flops 499258816 | bytes 63652156 | solution.py:126
  100.4 10.0 %while.20 = (s32[]{:T(128)}, bf16[1280,512]{1,0:T(8,128)(2,1)S(1)}, s32[4,2]{0,1:T(2,128)S(1)}, bf16[4,384,512]{1,2,0:T(8,128)(2,1)}, s32[]{:T(128)}) while((s32[]{:T(128)}, bf16[1280,512]{1,0:T(8,128)(2,1)S(1)}, s32[4,2]{0,1:T(2,128)S(1)}, bf16[4,384,512]{1,2,0:T(8,128)(2,1)}, s32[]{:T(128)}) %tuple.78), condition=%wide.while_cond, body=%wide.while_body.sunk | while | flops 2 | bytes 2359901 | solution.py:110
  112.5 2.8 %copy.78 = bf16[4,512,512]{1,2,0:T(8,128)(2,1)S(1)} copy(bf16[4,512,512]{2,1,0:T(8,128)(2,1)} %bitcast.149) | data formatting | bytes 4194304 | tf_op jit(solution)/shard_map/while/body/eval_jaxpr/vmap()/reshape | solution.py:111
  115.3 3.2 %pad_maximum_fusion.3 = (bf16[4,896,256]{1,2,0:T(8,128)(2,1)}, bf16[4,896,256]{1,2,0:T(8,128)(2,1)}) fusion(bf16[4,512,512]{1,2,0:T(8,128)(2,1)S(1)} %copy.78, bf16[4,384,512]{1,2,0:T(8,128)(2,1)} %get-tuple-element.282), kind=kLoop, calls=%fused_computation.31.clone.1 | loop fusion | flops 7340032 | bytes 7340032 | tf_op jit(solution)/shard_map/while/body/eval_jaxpr/vmap()/concatenate | solution.py:112
  118.5 9.7 %while.21 = (s32[]{:T(128)}, bf16[1024,256]{1,0:T(8,128)(2,1)}, s32[4,2]{0,1:T(2,128)S(1)}, bf16[4,128,256]{1,2,0:T(8,128)(2,1)S(1)}, s32[]{:T(128)}) while((s32[]{:T(128)}, bf16[1024,256]{1,0:T(8,128)(2,1)}, s32[4,2]{0,1:T(2,128)S(1)}, bf16[4,128,256]{1,2,0:T(8,128)(2,1)S(1)}, s32[]{:T(128)}) %tuple.81), condition=%wide.while_cond.1, body=%wide.while_body.1.sunk | while | flops 2 | bytes 393313 | solution.py:109
  128.3 9.3 %fusion.92 = (f32[4,8,128]{2,1,0:T(8,128)S(1)}, f32[4,8,128,896]{3,2,1,0:T(8,128)}) fusion(pred[4,896]{1,0:T(4,128)(4,1)S(1)} %bitcast_compare_fusion.2, bf16[4,128,8,32]{1,3,2,0:T(8,128)(2,1)S(1)} %bitcast.172, bf16[4,896,8,32]{1,3,2,0:T(8,128)(2,1)} %bitcast.151), kind=kOutput, calls=%fused_computation.154.clone.1 | convolution fusion | flops 249561984 | bytes 16797184 | tf_op jit(solution)/shard_map/while/body/eval_jaxpr/vmap()/sub | solution.py:45
  137.6 8.5 %fusion.93 = bf16[4,8,32,128]{3,2,1,0:T(8,128)(2,1)S(1)} fusion(bf16[4,896,8,32]{1,3,2,0:T(8,128)(2,1)} %bitcast.150, f32[4,8,128,896]{3,2,1,0:T(8,128)} %get-tuple-element.287, f32[4,8,128]{2,1,0:T(8,128)S(1)} %get-tuple-element.288), kind=kOutput, calls=%fused_computation.33.clone.1 | convolution fusion | flops 242352128 | bytes 16793600 | tf_op jit(solution)/shard_map/while/body/eval_jaxpr/vmap(hqk,khd->qhd)/dot_general | solution.py:48
  147.7 10.0 %while.20 = (s32[]{:T(128)}, bf16[1280,512]{1,0:T(8,128)(2,1)S(1)}, s32[4,2]{0,1:T(2,128)S(1)}, bf16[4,384,512]{1,2,0:T(8,128)(2,1)}, s32[]{:T(128)}) while((s32[]{:T(128)}, bf16[1280,512]{1,0:T(8,128)(2,1)S(1)}, s32[4,2]{0,1:T(2,128)S(1)}, bf16[4,384,512]{1,2,0:T(8,128)(2,1)}, s32[]{:T(128)}) %tuple.78), condition=%wide.while_cond, body=%wide.while_body.sunk | while | flops 2 | bytes 2359901 | solution.py:110
  162.6 3.2 %pad_maximum_fusion.3 = (bf16[4,896,256]{1,2,0:T(8,128)(2,1)}, bf16[4,896,256]{1,2,0:T(8,128)(2,1)}) fusion(bf16[4,512,512]{1,2,0:T(8,128)(2,1)S(1)} %copy.78, bf16[4,384,512]{1,2,0:T(8,128)(2,1)} %get-tuple-element.282), kind=kLoop, calls=%fused_computation.31.clone.1 | loop fusion | flops 7340032 | bytes 7340032 | tf_op jit(solution)/shard_map/while/body/eval_jaxpr/vmap()/concatenate | solution.py:112
  165.8 9.7 %while.21 = (s32[]{:T(128)}, bf16[1024,256]{1,0:T(8,128)(2,1)}, s32[4,2]{0,1:T(2,128)S(1)}, bf16[4,128,256]{1,2,0:T(8,128)(2,1)S(1)}, s32[]{:T(128)}) while((s32[]{:T(128)}, bf16[1024,256]{1,0:T(8,128)(2,1)}, s32[4,2]{0,1:T(2,128)S(1)}, bf16[4,128,256]{1,2,0:T(8,128)(2,1)S(1)}, s32[]{:T(128)}) %tuple.81), condition=%wide.while_cond.1, body=%wide.while_body.1.sunk | while | flops 2 | bytes 393313 | solution.py:109
  175.5 9.3 %fusion.92 = (f32[4,8,128]{2,1,0:T(8,128)S(1)}, f32[4,8,128,896]{3,2,1,0:T(8,128)}) fusion(pred[4,896]{1,0:T(4,128)(4,1)S(1)} %bitcast_compare_fusion.2, bf16[4,128,8,32]{1,3,2,0:T(8,128)(2,1)S(1)} %bitcast.172, bf16[4,896,8,32]{1,3,2,0:T(8,128)(2,1)} %bitcast.151), kind=kOutput, calls=%fused_computation.154.clone.1 | convolution fusion | flops 249561984 | bytes 16797184 | tf_op jit(solution)/shard_map/while/body/eval_jaxpr/vmap()/sub | solution.py:45
  184.8 8.5 %fusion.93 = bf16[4,8,32,128]{3,2,1,0:T(8,128)(2,1)S(1)} fusion(bf16[4,896,8,32]{1,3,2,0:T(8,128)(2,1)} %bitcast.150, f32[4,8,128,896]{3,2,1,0:T(8,128)} %get-tuple-element.287, f32[4,8,128]{2,1,0:T(8,128)S(1)} %get-tuple-element.288), kind=kOutput, calls=%fused_computation.33.clone.1 | convolution fusion | flops 242352128 | bytes 16793600 | tf_op jit(solution)/shard_map/while/body/eval_jaxpr/vmap(hqk,khd->qhd)/dot_general | solution.py:48
  (237 shorter events, 89.3 us)
Async XLA Ops:
  0.0 61.0 %copy-start = (bf16[256,768]{1,0:T(8,128)(2,1)S(1)}, bf16[256,768]{1,0:T(8,128)(2,1)}, u32[]{:S(2)}) copy-start(bf16[256,768]{1,0:T(8,128)(2,1)} %param.26) | copy-start | bytes 1179652
  0.0 16.5 %copy-start.6 = (bf16[1,1024,256]{2,1,0:T(8,128)(2,1)S(1)}, bf16[1,1024,256]{2,1,0:T(8,128)(2,1)}, u32[]{:S(2)}) copy-start(bf16[1,1024,256]{2,1,0:T(8,128)(2,1)} %param.16) | copy-start | bytes 1572868
  0.0 14.8 %copy-start.14 = (s32[1,1024,6]{1,0,2:T(1,128)S(1)}, s32[1,1024,6]{1,0,2:T(1,128)}, u32[]{:S(2)}) copy-start(s32[1,1024,6]{1,0,2:T(1,128)} %param.18) | copy-start | bytes 73732
  3.7 17.9 %collective-permute-start.2 = (bf16[256,256]{0,1:T(8,128)(2,1)S(1)}, bf16[256,256]{0,1:T(8,128)(2,1)S(1)}, u32[]{:S(2)}, u32[]{:S(2)}) collective-permute-start(bf16[256,256]{0,1:T(8,128)(2,1)S(1)} %copy.42), channel_id=1, source_target_pairs={{0,8},{8,16},{16,24},{1,9},{9,17},{17,25},{2,10},{10,18},{18,26},{... | collective-permute-start | bytes 393224 | tf_op jit(solution)/shard_map/ppermute | solution.py:20
  5.4 17.6 %collective-permute-start.3 = (bf16[256,256]{0,1:T(8,128)(2,1)S(1)}, bf16[256,256]{0,1:T(8,128)(2,1)S(1)}, u32[]{:S(2)}, u32[]{:S(2)}) collective-permute-start(bf16[256,256]{0,1:T(8,128)(2,1)S(1)} %copy.42), channel_id=1, source_target_pairs={{8,0},{16,8},{24,16},{9,1},{17,9},{25,17},{10,2},{18,10},{26,18},{... | collective-permute-start | bytes 393224 | tf_op jit(solution)/shard_map/ppermute | solution.py:23
  8.0 11.3 %collective-permute-start = (bf16[128,256]{0,1:T(8,128)(2,1)S(1)}, bf16[128,256]{0,1:T(8,128)(2,1)S(1)}, u32[]{:S(2)}, u32[]{:S(2)}) collective-permute-start(bf16[128,256]{0,1:T(8,128)(2,1)S(1)} %get-tuple-element.147), channel_id=1, source_target_pairs={{0,1},{1,2},{2,3},{3,4},{4,5},{5,6},{6,7},{8,9},{9,10},{10,11},{11... | collective-permute-start | bytes 196616 | tf_op jit(solution)/shard_map/ppermute | solution.py:20
  11.4 9.5 %collective-permute-start.1 = (bf16[128,256]{0,1:T(8,128)(2,1)S(1)}, bf16[128,256]{0,1:T(8,128)(2,1)S(1)}, u32[]{:S(2)}, u32[]{:S(2)}) collective-permute-start(bf16[128,256]{0,1:T(8,128)(2,1)S(1)} %get-tuple-element.146), channel_id=1, source_target_pairs={{1,0},{2,1},{3,2},{4,3},{5,4},{6,5},{7,6},{9,8},{10,9},{11,10},{12... | collective-permute-start | bytes 196616 | tf_op jit(solution)/shard_map/ppermute | solution.py:23
  54.6 2.0 %copy-start.11 = (bf16[1024,256]{1,0:T(8,128)(2,1)S(1)}, bf16[1024,256]{1,0:T(8,128)(2,1)}, u32[]{:S(2)}) copy-start(bf16[1024,256]{1,0:T(8,128)(2,1)} %gather_fusion.7) | copy-start | bytes 1572868
  54.6 2.1 %copy-start.13 = (bf16[7,256,256]{2,1,0:T(8,128)(2,1)S(1)}, bf16[7,256,256]{2,1,0:T(8,128)(2,1)}, u32[]{:S(2)}) copy-start(bf16[7,256,256]{2,1,0:T(8,128)(2,1)} %param.22) | copy-start | bytes 2752516
  54.6 2.1 %copy-start.17 = (pred[1024]{0:T(1024)(128)(4,1)S(1)}, pred[1024]{0:T(1024)(128)(4,1)}, u32[]{:S(2)}) copy-start(pred[1024]{0:T(1024)(128)(4,1)} %compare_and_fusion.4) | copy-start | bytes 3076
  56.7 1.0 copy-start.10
  61.9 1.2 copy-start.7
  63.1 1.6 copy-start.5
  63.1 6.8 %copy-start.19 = (s32[1,8,8]{2,1,0:T(8,128)S(1)}, s32[1,8,8]{2,1,0:T(8,128)}, u32[]{:S(2)}) copy-start(s32[1,8,8]{2,1,0:T(8,128)} %param.21) | copy-start | bytes 772
  63.1 7.0 %copy-start.15 = (s32[1,8,4]{1,2,0:T(4,128)S(1)}, s32[1,8,4]{1,2,0:T(4,128)}, u32[]{:S(2)}) copy-start(s32[1,8,4]{1,2,0:T(4,128)} %param.20) | copy-start | bytes 388
  64.7 35.0 %all-to-all-start = ((bf16[8,128,512]{2,1,0:T(8,128)(2,1)}), bf16[8,128,512]{2,1,0:T(8,128)(2,1)S(1)}, u32[]{:S(2)}, u32[]{:S(2)}) async-start(bf16[8,128,512]{2,1,0:T(8,128)(2,1)} %gather_fusion.2), calls=%async_computation | async-start | bytes 2097152 | tf_op jit(solution)/shard_map/all_to_all | solution.py:96
  70.3 1.8 copy-start.8
  70.3 9.5 %copy-start.1 = (s32[1,64]{1,0:T(1,128)S(1)}, s32[1,64]{1,0:T(1,128)}, u32[]{:S(2)}) copy-start(s32[1,64]{1,0:T(1,128)} %param.19) | copy-start | bytes 772
  72.1 26.2 %collective-permute-start.4 = (bf16[128,512]{1,0:T(8,128)(2,1)S(1)}, bf16[128,512]{1,0:T(8,128)(2,1)S(1)}, u32[]{:S(2)}, u32[]{:S(2)}) collective-permute-start(bf16[128,512]{1,0:T(8,128)(2,1)S(1)} %get-tuple-element.144), channel_id=1, source_target_pairs={{0,1},{1,2},{2,3},{3,4},{4,5},{5,6},{6,7},{8,9},{9,10},{10,11},{11... | collective-permute-start | bytes 393224 | tf_op jit(solution)/shard_map/ppermute | solution.py:20
  75.5 22.9 %collective-permute-start.5 = (bf16[128,512]{1,0:T(8,128)(2,1)S(1)}, bf16[128,512]{1,0:T(8,128)(2,1)S(1)}, u32[]{:S(2)}, u32[]{:S(2)}) collective-permute-start(bf16[128,512]{1,0:T(8,128)(2,1)S(1)} %get-tuple-element.145), channel_id=1, source_target_pairs={{1,0},{2,1},{3,2},{4,3},{5,4},{6,5},{7,6},{9,8},{10,9},{11,10},{12... | collective-permute-start | bytes 393224 | tf_op jit(solution)/shard_map/ppermute | solution.py:23
  110.4 2.1 %copy-start.2 = (bf16[1280,512]{1,0:T(8,128)(2,1)}, bf16[1280,512]{1,0:T(8,128)(2,1)S(1)}, u32[]{:S(2)}) copy-start(bf16[1280,512]{1,0:T(8,128)(2,1)S(1)} %get-tuple-element.365) | copy-start | bytes 3932164 | tf_op jit(solution)/shard_map/while
  137.6 9.4 %copy-start.3 = (bf16[1280,512]{1,0:T(8,128)(2,1)S(1)}, bf16[1280,512]{1,0:T(8,128)(2,1)}, u32[]{:S(2)}) copy-start(bf16[1280,512]{1,0:T(8,128)(2,1)} %copy-done.2) | copy-start | bytes 3932164 | tf_op jit(solution)/shard_map/while
  157.7 2.1 %copy-start.2 = (bf16[1280,512]{1,0:T(8,128)(2,1)}, bf16[1280,512]{1,0:T(8,128)(2,1)S(1)}, u32[]{:S(2)}) copy-start(bf16[1280,512]{1,0:T(8,128)(2,1)S(1)} %get-tuple-element.365) | copy-start | bytes 3932164 | tf_op jit(solution)/shard_map/while
  184.8 9.4 %copy-start.3 = (bf16[1280,512]{1,0:T(8,128)(2,1)S(1)}, bf16[1280,512]{1,0:T(8,128)(2,1)}, u32[]{:S(2)}) copy-start(bf16[1280,512]{1,0:T(8,128)(2,1)} %copy-done.2) | copy-start | bytes 3932164 | tf_op jit(solution)/shard_map/while
  (8 other events, 7.7 us)
where the time goes:
time: 199 us; the launch traced here: 197 us
  local copies, waits for them, and re-layouts  99.7 us (50%)
  matrix products  45 us (23%)
  starting transfers between devices  21.9 us (11%)
  other arithmetic  15 us (8%)
  waiting for transfers between devices  14.6 us (7%)
    gather x80, local copies, waits for them, and re-layouts  38.9 us
    gather x6, local copies, waits for them, and re-layouts, on_device(): offset_rows = jnp.take(neighbour_table, offset_ids[offset], axis=0)  28.7 us
    sub x2, matrix products, attend(): raw_weights = jnp.exp(scores - row_peak)  18.6 us
    dot_general x2, matrix products, attend(): jnp.einsum('hqk,khd->qhd', attn_weights, value_heads, preferred_element_t...  17.1 us
    ppermute x3, waiting for transfers between devices, extended(): lax.ppermute(lax.slice_in_dim(block, block.shape[dim] - width, None, axis...  14.6 us
    ppermute x3, starting transfers between devices, extended(): lax.ppermute(lax.slice_in_dim(block, block.shape[dim] - width, None, axis...  8.52 us
    unnamed x51, local copies, waits for them, and re-layouts  8.44 us
    ppermute x3, starting transfers between devices, extended(): lax.ppermute(lax.slice_in_dim(block, 0, width, axis=dim), axis, backward)  8.18 us
  transfers between devices with their start and end apart: 7, of which 1 were waited for; matrix products, arithmetic and copies ran while one was open for 9% of the time, Pallas kernels for 0%

commit v1 on v0

v1 whole, which is shorter than its diff:
```python
import math

import jax
import jax.numpy as jnp
from jax import lax
from jax.experimental import pallas as pl
from jax.experimental.pallas import tpu as pltpu
from jax.sharding import PartitionSpec as P

D = 256
HEADS = 8
BLK = 128
EDGE = 128
FACE = 256


def extended(block, sides, width):
    for axis, dim in sides:
        count = lax.axis_size(axis)
        forward = [(i, i + 1) for i in range(count - 1)]
        backward = [(target, source) for source, target in forward]
        low = lax.ppermute(
            lax.slice_in_dim(block, block.shape[dim] - width, None, axis=dim), axis, forward
        )
        high = lax.ppermute(lax.slice_in_dim(block, 0, width, axis=dim), axis, backward)
        block = jnp.concatenate([low, block, high], axis=dim)
    return block


ROWS = 256


def encode_kernel(
    ids_ref, own_ref, table_ref, weight_ref, bias_ref, gain_ref, shift_ref, qkv_ref,
    hidden_ref, query_ref, kv_ref,
):
    rows = own_ref.shape[0]
    count = table_ref.shape[0]
    own = own_ref[...]
    conv = jnp.dot(own, weight_ref[0], preferred_element_type=jnp.float32)
    lane = lax.broadcasted_iota(jnp.int32, (rows, 128), 1)
    ids = ids_ref[...]
    for offset in range(6):
        column = jnp.broadcast_to(ids[:, offset : offset + 1], (rows, 128))
        low = column & 127
        high = (column >> 7).astype(jnp.float32).astype(jnp.bfloat16)
        hot = jnp.where(low == lane, 1.0, 0.0).astype(jnp.bfloat16)
        zero = jnp.zeros_like(hot)
        chosen = jnp.concatenate(
            [jnp.where(high == jnp.bfloat16(part), hot, zero) for part in range(count // 128)], 1
        )
        picked = jnp.dot(chosen, table_ref[...], preferred_element_type=jnp.float32)
        conv = conv + jnp.dot(
            picked.astype(jnp.bfloat16), weight_ref[offset + 1], preferred_element_type=jnp.float32
        )
    hidden = own.astype(jnp.float32) + conv + bias_ref[...]
    hidden_ref[...] = hidden
    center = hidden - jnp.mean(hidden, axis=-1, keepdims=True)
    variance = jnp.mean(center * center, axis=-1, keepdims=True)
    normed = (center * lax.rsqrt(variance + 1e-05) * gain_ref[...] + shift_ref[...]).astype(jnp.bfloat16)
    projected = jnp.dot(normed, qkv_ref[...], preferred_element_type=jnp.float32).astype(jnp.bfloat16)
    query_ref[...] = projected[:, :D]
    kv_ref[...] = projected[:, D:]


def encode(ids, own, table, weight, bias, gain, shift, w_qkv):
    count, width = own.shape
    whole = lambda shape: pl.BlockSpec(shape, lambda i: (0,) * len(shape))
    tile = lambda cols: pl.BlockSpec((ROWS, cols), lambda i: (i, 0))
    return pl.pallas_call(
        encode_kernel,
        grid=(count // ROWS,),
        in_specs=[
            tile(6), tile(width), whole(table.shape), whole(weight.shape),
            whole((1, width)), whole((1, width)), whole((1, width)), whole(w_qkv.shape),
        ],
        out_specs=[tile(width), tile(width), tile(2 * width)],
        out_shape=[
            jax.ShapeDtypeStruct((count, width), jnp.float32),
            jax.ShapeDtypeStruct((count, width), jnp.bfloat16),
            jax.ShapeDtypeStruct((count, 2 * width), jnp.bfloat16),
        ],
        compiler_params=pltpu.CompilerParams(vmem_limit_bytes=40 * 2**20),
    )(ids, own, table, weight, bias[None], gain[None], shift[None], w_qkv)


GROUP = 4


def attend_kernel(
    slots_ref, lens_ref, query_ref, window_ref, remote_ref, hidden_ref, out_w_ref, out_ref, kv_ref
):
    blk = pl.program_id(0)
    start = pl.multiple_of(blk * BLK, BLK)
    kv_ref[0 : 3 * BLK, :] = window_ref[pl.ds(start, 3 * BLK), :]
    for slot in range(4):
        where = pl.multiple_of(slots_ref[blk, slot] * BLK, BLK)
        kv_ref[(3 + slot) * BLK : (4 + slot) * BLK, :] = remote_ref[pl.ds(where, BLK), :]
    lane = lax.broadcasted_iota(jnp.int32, (1, BLK), 1)
    mask = jnp.concatenate(
        [jnp.where(lane < lens_ref[blk, part], 0.0, -1e30) for part in range(7)], 1
    )
    head_dim = D // HEADS
    head_of = lax.broadcasted_iota(jnp.int32, (BLK, D), 1) // head_dim
    query = query_ref[...]
    keys = kv_ref[:, :D]
    values = kv_ref[:, D:]
    scale = 1.0 / math.sqrt(head_dim)
    attended = jnp.zeros((BLK, D), jnp.float32)
    for group in range(0, HEADS, GROUP):
        stacked = jnp.concatenate(
            [jnp.where(head_of == head, query, jnp.zeros_like(query)) for head in range(group, group + GROUP)], 0
        )
        scores = lax.dot_general(
            stacked, keys, (((1,), (1,)), ((), ())), preferred_element_type=jnp.float32
        ) * scale + mask
        raw = jnp.exp(scores - jnp.max(scores, axis=-1, keepdims=True))
        inverse = 1.0 / jnp.sum(raw, axis=-1, keepdims=True)
        weights = (raw * inverse).astype(jnp.bfloat16)
        mixed = jnp.dot(weights, values, preferred_element_type=jnp.float32)
        for part in range(GROUP):
            attended = jnp.where(head_of == group + part, mixed[part * BLK : (part + 1) * BLK], attended)
    out = hidden_ref[...] + jnp.dot(
        attended.astype(jnp.bfloat16), out_w_ref[...], preferred_element_type=jnp.float32
    )
    out_ref[...] = out.astype(jnp.bfloat16)


def attend(slots, lens, queries, window, remote, hidden, w_out):
    count, width = queries.shape
    whole = lambda shape: pl.BlockSpec(shape, lambda i, *_: (0,) * len(shape))
    tile = pl.BlockSpec((BLK, width), lambda i, *_: (i, 0))
    return pl.pallas_call(
        attend_kernel,
        grid_spec=pltpu.PrefetchScalarGridSpec(
            num_scalar_prefetch=2,
            grid=(count // BLK,),
            in_specs=[tile, whole(window.shape), whole(remote.shape), tile, whole(w_out.shape)],
            out_specs=tile,
            scratch_shapes=[pltpu.VMEM((7 * BLK, 2 * width), jnp.bfloat16)],
        ),
        out_shape=jax.ShapeDtypeStruct((count, width), jnp.bfloat16),
        compiler_params=pltpu.CompilerParams(vmem_limit_bytes=48 * 2**20),
    )(slots, lens, queries, window, remote, hidden, w_out)


def on_device(
    feats,
    face_rows,
    neighbours,
    block_len,
    dilated,
    pick,
    cpe_weight,
    cpe_bias,
    ln_gain,
    ln_bias,
    w_qkv,
    w_out,
):
    voxels = feats[0]
    count_vox = voxels.shape[0]
    feat_width = voxels.shape[1]
    blocks_dev = count_vox // BLK
    my_range = lax.axis_index("ctx")
    edge_rows = extended(voxels, (("ctx", 0),), EDGE)
    face_out = voxels[face_rows[0]]
    face_all = extended(face_out, (("space", 0),), FACE)
    neighbour_table = jnp.concatenate([edge_rows, face_all], 0)
    hidden, queries, key_value = encode(
        neighbours[0], voxels, neighbour_table, cpe_weight, cpe_bias, ln_gain, ln_bias, w_qkv
    )
    window_kv = extended(key_value, (("ctx", 0),), BLK)
    pick_tile = pick[0]
    send_index = pick_tile[my_range]
    recv_index = pick_tile[:, my_range]
    outgoing = key_value.reshape(blocks_dev, BLK, 2 * feat_width)[send_index]
    remote_kv = lax.all_to_all(outgoing, "ctx", split_axis=0, concat_axis=0, tiled=True)
    lens_tile = block_len[0]
    lens_ext = jnp.pad(lens_tile, (1, 1))
    local_ids = jnp.arange(blocks_dev, dtype=jnp.int32)
    global_ids = my_range * blocks_dev + local_ids
    win_lens = lens_ext[global_ids[:, None] + jnp.arange(3, dtype=jnp.int32)[None, :]]
    slot_ids = dilated[0]
    far_ids = slot_ids * blocks_dev + recv_index[slot_ids]
    far_lens = lens_tile[far_ids]
    key_lens = jnp.concatenate([win_lens, far_lens], 1)
    output = attend(
        slot_ids, key_lens, queries, window_kv, remote_kv.reshape(-1, 2 * feat_width), hidden, w_out
    )
    return output[None]


def solution(mesh):
    placed = (
        P("space", "ctx", None),
        P("space", "ctx"),
        P("space", "ctx", None),
        P("space", None),
        P("space", "ctx", None),
        P("space", None, None),
        P(),
        P(),
        P(),
        P(),
        P(),
        P(),
    )
    return jax.shard_map(
        on_device, mesh=mesh, in_specs=placed, out_specs=P("space", "ctx", None), check_vma=False
    )
```

time: 199 us -> 94.9 us (0.48)
  local copies, waits for them, and re-layouts: 99.7 us -> 11.4 us
  matrix products: 45 us -> 0 us
  Pallas kernels: 0 us -> 38 us
  other arithmetic: 15 us -> 1.61 us
  waiting for transfers between devices: 14.6 us -> 20 us
    gather x88 -> x0, local copies, waits for them, and re-layouts: 71.6 us -> none
    pallas_call x0 -> x2, Pallas kernels: none -> 38 us  [the longest x1 24.2 us: attend(): pl.pallas_call(attend_kernel, grid_spec=pltpu.PrefetchScalarGridSpec(num_...]
    dot_general x11 -> x0, matrix products: 26.4 us -> none  [the longest x2 17.1 us: attend(): jnp.einsum('hqk,khd->qhd', attn_weights, value_heads, preferred_element_t...]
    sub x2 -> x0, matrix products: 18.6 us -> none  [attend(): raw_weights = jnp.exp(scores - row_peak)]
    concatenate x2 -> x0, other arithmetic: 6.33 us -> none  [one_block(): keys_all = jnp.concatenate([window_rows, remote_rows], 0)]
    reshape x2 -> x0, local copies, waits for them, and re-layouts: 5.57 us -> none  [one_block(): remote_rows = remote_kv[slot_row].reshape(-1, 2 * feat_width)]
    ppermute x3, waiting for transfers between devices: 14.6 us -> 19.6 us  [extended(): lax.ppermute(lax.slice_in_dim(block, block.shape[dim] - width, None, axis...]
    unnamed x51 -> x34, local copies, waits for them, and re-layouts: 8.44 us -> 3.54 us
  transfers between devices with their start and end apart: 7 -> 7, of which waited for: 1 -> 2; matrix products, arithmetic and copies ran while one was open for 9% -> 6% of each run, Pallas kernels for 0% -> 0%
where the time goes in v1:
time: 94.9 us; the launch traced here: 94 us
  Pallas kernels  38 us (40%)
  starting transfers between devices  22.7 us (24%)
  waiting for transfers between devices  20 us (21%)
  local copies, waits for them, and re-layouts  11.4 us (12%)
  other arithmetic  1.61 us (2%)
    pallas_call x1, Pallas kernels, attend(): pl.pallas_call(attend_kernel, grid_spec=pltpu.PrefetchScalarGridSpec(num_...  24.2 us
    ppermute x3, waiting for transfers between devices, extended(): lax.ppermute(lax.slice_in_dim(block, block.shape[dim] - width, None, axis...  19.6 us
    pallas_call x1, Pallas kernels, encode(): pl.pallas_call(encode_kernel, grid=(count // ROWS,), in_specs=[tile(6), t...  13.8 us
    ppermute x3, starting transfers between devices, extended(): lax.ppermute(lax.slice_in_dim(block, block.shape[dim] - width, None, axis...  8.52 us
    ppermute x3, starting transfers between devices, extended(): lax.ppermute(lax.slice_in_dim(block, 0, width, axis=dim), axis, backward)  8 us
    all_to_all x1, starting transfers between devices, on_device(): lax.all_to_all(outgoing, 'ctx', split_axis=0, concat_axis=0, tiled=True)  6.21 us
    unnamed x34, local copies, waits for them, and re-layouts  3.54 us
    gather x1, local copies, waits for them, and re-layouts, on_device(): face_out = voxels[face_rows[0]]  2.07 us
  transfers between devices with their start and end apart: 7, of which 2 were waited for; matrix products, arithmetic and copies ran while one was open for 6% of the time, Pallas kernels for 0%

profile of v1, /device:TPU:16, one launch (start us, length us, event | category | flops | bytes accessed | tf_op | source)
XLA Modules:
  0.0 94.0 jit_solution(18389978891753178400)
XLA Ops:
  0.0 0.7 compare_select_fusion.1
  0.7 2.1 %gather_fusion.3 = bf16[256,256]{1,0:T(8,128)(2,1)S(1)} fusion(bf16[1024,256]{1,0:T(8,128)(2,1)} %bitcast.35, s32[1024]{0:T(1024)S(1)} %pad_clamp_fusion.1), kind=kCustom, calls=%fused_computation.3 | custom fusion | bytes 263168 | tf_op jit(solution)/shard_map/gather | solution.py:167
  2.8 1.7 %collective-permute-start.2 = (bf16[256,256]{1,0:T(8,128)(2,1)S(1)}, bf16[256,256]{1,0:T(8,128)(2,1)S(1)}, u32[]{:S(2)}, u32[]{:S(2)}) collective-permute-start(bf16[256,256]{1,0:T(8,128)(2,1)S(1)} %gather_fusion.3), channel_id=1, source_target_pairs={{0,8},{8,16},{16,24},{1,9},{9,17},{17,25},{2,10},{10,18},{18,26},{... | collective-permute-start | bytes 393224 | tf_op jit(solution)/shard_map/ppermute | solution.py:22
  4.6 1.3 %collective-permute-start.3 = (bf16[256,256]{1,0:T(8,128)(2,1)S(1)}, bf16[256,256]{1,0:T(8,128)(2,1)S(1)}, u32[]{:S(2)}, u32[]{:S(2)}) collective-permute-start(bf16[256,256]{1,0:T(8,128)(2,1)S(1)} %gather_fusion.3), channel_id=1, source_target_pairs={{8,0},{16,8},{24,16},{9,1},{17,9},{25,17},{10,2},{18,10},{26,18},{... | collective-permute-start | bytes 393224 | tf_op jit(solution)/shard_map/ppermute | solution.py:25
  5.9 0.9 slice_bitcast_fusion
  6.8 3.4 %collective-permute-start = (bf16[128,256]{1,0:T(8,128)(2,1)S(1)}, bf16[128,256]{1,0:T(8,128)(2,1)S(1)}, u32[]{:S(2)}, u32[]{:S(2)}) collective-permute-start(bf16[128,256]{1,0:T(8,128)(2,1)S(1)} %get-tuple-element.14), channel_id=1, source_target_pairs={{0,1},{1,2},{2,3},{3,4},{4,5},{5,6},{6,7},{8,9},{9,10},{10,11},{11... | collective-permute-start | bytes 196616 | tf_op jit(solution)/shard_map/ppermute | solution.py:22
  10.2 3.3 %collective-permute-start.1 = (bf16[128,256]{1,0:T(8,128)(2,1)S(1)}, bf16[128,256]{1,0:T(8,128)(2,1)S(1)}, u32[]{:S(2)}, u32[]{:S(2)}) collective-permute-start(bf16[128,256]{1,0:T(8,128)(2,1)S(1)} %get-tuple-element.13), channel_id=1, source_target_pairs={{1,0},{2,1},{3,2},{4,3},{5,4},{6,5},{7,6},{9,8},{10,9},{11,10},{12... | collective-permute-start | bytes 196616 | tf_op jit(solution)/shard_map/ppermute | solution.py:25
  13.5 0.2 dynamic-slice_reduce_fusion
  13.7 0.2 copy.21
  14.2 0.7 gather_fusion.1
  15.2 0.6 pad_clamp_fusion
  15.9 0.4 collective-permute-done.1
  16.5 1.0 %copy-done.4 = bf16[256,768]{1,0:T(8,128)(2,1)S(1)} copy-done((bf16[256,768]{1,0:T(8,128)(2,1)S(1)}, bf16[256,768]{1,0:T(8,128)(2,1)}, u32[]{:S(2)}) %copy-start.4) | copy-done | bytes 393240
  17.4 13.8 %shard_map.118 = (f32[1024,256]{1,0:T(8,128)S(1)}, bf16[1024,256]{1,0:T(8,128)(2,1)S(1)}, bf16[1024,512]{1,0:T(8,128)(2,1)S(1)}) custom-call(s32[1024,6]{1,0:T(8,128)S(1)} %bitcast.38, bf16[1024,256]{1,0:T(8,128)(2,1)S(1)} %bitcast.36, bf16[2048,256]{1,0:T(8,128)(2,1)S(1)} %constant_dynamic-update-slice_fusion.table_ref, bf16[7,256,256]{2,1,0:T(8,128)(2,1)S(1)} %copy-done.3, ...), custom_call_target="tpu_custom_call" | custom-call | tf_op jit(solution)/shard_map/pallas_call | solution.py:70
  31.2 1.0 %copy-done.1 = f32[1024,256]{1,0:T(8,128)} copy-done((f32[1024,256]{1,0:T(8,128)}, f32[1024,256]{1,0:T(8,128)S(1)}, u32[]{:S(2)}) %copy-start.1) | copy-done | bytes 1048600
  32.2 1.7 %gather_fusion.4 = bf16[8,128,512]{2,1,0:T(8,128)(2,1)} fusion(bf16[8,128,512]{2,1,0:T(8,128)(2,1)S(1)} %bitcast.37, s32[1024]{0:T(1024)} %get-tuple-element.15), kind=kCustom, calls=%fused_computation.4 | custom fusion | bytes 2097184 | tf_op jit(solution)/shard_map/gather | solution.py:177
  34.0 6.2 %all-to-all-start = ((bf16[8,128,512]{2,1,0:T(8,128)(2,1)}), bf16[8,128,512]{2,1,0:T(8,128)(2,1)}, u32[]{:S(2)}, u32[]{:S(2)}) async-start(bf16[8,128,512]{2,1,0:T(8,128)(2,1)} %gather_fusion.4), calls=%async_computation | async-start | bytes 2097152 | tf_op jit(solution)/shard_map/all_to_all | solution.py:178
  40.3 3.4 %collective-permute-start.4 = (bf16[128,512]{1,0:T(8,128)(2,1)S(1)}, bf16[128,512]{1,0:T(8,128)(2,1)S(1)}, u32[]{:S(2)}, u32[]{:S(2)}) collective-permute-start(bf16[128,512]{1,0:T(8,128)(2,1)S(1)} %get-tuple-element.11), channel_id=1, source_target_pairs={{0,1},{1,2},{2,3},{3,4},{4,5},{5,6},{6,7},{8,9},{9,10},{10,11},{11... | collective-permute-start | bytes 393224 | tf_op jit(solution)/shard_map/ppermute | solution.py:22
  43.7 3.4 %collective-permute-start.5 = (bf16[128,512]{1,0:T(8,128)(2,1)S(1)}, bf16[128,512]{1,0:T(8,128)(2,1)S(1)}, u32[]{:S(2)}, u32[]{:S(2)}) collective-permute-start(bf16[128,512]{1,0:T(8,128)(2,1)S(1)} %get-tuple-element.12), channel_id=1, source_target_pairs={{1,0},{2,1},{3,2},{4,3},{5,4},{6,5},{7,6},{9,8},{10,9},{11,10},{12... | collective-permute-start | bytes 393224 | tf_op jit(solution)/shard_map/ppermute | solution.py:25
  47.2 0.7 gather_fusion.2
  48.0 0.7 gather_fusion
  48.9 19.6 %collective-permute-done.4 = bf16[128,512]{1,0:T(8,128)(2,1)S(1)} collective-permute-done((bf16[128,512]{1,0:T(8,128)(2,1)S(1)}, bf16[128,512]{1,0:T(8,128)(2,1)S(1)}, u32[]{:S(2)}, u32[]{:S(2)}) %collective-permute-start.4) | collective-permute-done | bytes 131104 | tf_op jit(solution)/shard_map/ppermute | solution.py:22
  68.6 1.2 %copy-done.2 = f32[1024,256]{1,0:T(8,128)S(1)} copy-done((f32[1024,256]{1,0:T(8,128)S(1)}, f32[1024,256]{1,0:T(8,128)}, u32[]{:S(2)}) %copy-start.2) | copy-done | bytes 1048600
  69.8 24.2 %shard_map.119 = bf16[1024,256]{1,0:T(8,128)(2,1)} custom-call(s32[8,4]{1,0:T(8,128)S(1)} %copy.22.slots_ref, s32[8,7]{1,0:T(8,128)S(1)} %pad_add_fusion.lens_ref, bf16[1024,256]{1,0:T(8,128)(2,1)S(1)} %get-tuple-element.8.query_ref, bf16[1280,512]{1,0:T(8,128)(2,1)S(1)} %pad_maximum_fusion.window_ref, bf16[1024,512]{1,0:T(8,128)(2,1)} %bitcast.15.remote_ref, ...), custom_call_target="tpu_custom_call" | custom-call | tf_op jit(solution)/shard_map/pallas_call | solution.py:133
  (58 shorter events, 1.3 us)
Async XLA Ops:
  0.0 13.5 %copy-start.13 = (s32[1,8,8]{2,1,0:T(8,128)S(1)}, s32[1,8,8]{2,1,0:T(8,128)}, u32[]{:S(2)}) copy-start(s32[1,8,8]{2,1,0:T(8,128)} %param.17) | copy-start | bytes 772
  0.0 13.7 %copy-start.10 = (s32[1,1024,6]{1,0,2:T(1,128)S(1)}, s32[1,1024,6]{1,0,2:T(1,128)}, u32[]{:S(2)}) copy-start(s32[1,1024,6]{1,0,2:T(1,128)} %param.14) | copy-start | bytes 73732
  0.0 14.0 %copy-start.11 = (s32[1,8,4]{1,2,0:T(4,128)S(1)}, s32[1,8,4]{1,2,0:T(4,128)}, u32[]{:S(2)}) copy-start(s32[1,8,4]{1,2,0:T(4,128)} %param.16) | copy-start | bytes 388
  2.8 13.5 %collective-permute-start.2 = (bf16[256,256]{1,0:T(8,128)(2,1)S(1)}, bf16[256,256]{1,0:T(8,128)(2,1)S(1)}, u32[]{:S(2)}, u32[]{:S(2)}) collective-permute-start(bf16[256,256]{1,0:T(8,128)(2,1)S(1)} %gather_fusion.3), channel_id=1, source_target_pairs={{0,8},{8,16},{16,24},{1,9},{9,17},{17,25},{2,10},{10,18},{18,26},{... | collective-permute-start | bytes 393224 | tf_op jit(solution)/shard_map/ppermute | solution.py:22
  4.6 11.8 %collective-permute-start.3 = (bf16[256,256]{1,0:T(8,128)(2,1)S(1)}, bf16[256,256]{1,0:T(8,128)(2,1)S(1)}, u32[]{:S(2)}, u32[]{:S(2)}) collective-permute-start(bf16[256,256]{1,0:T(8,128)(2,1)S(1)} %gather_fusion.3), channel_id=1, source_target_pairs={{8,0},{16,8},{24,16},{9,1},{17,9},{25,17},{10,2},{18,10},{26,18},{... | collective-permute-start | bytes 393224 | tf_op jit(solution)/shard_map/ppermute | solution.py:25
  6.8 9.1 %collective-permute-start = (bf16[128,256]{1,0:T(8,128)(2,1)S(1)}, bf16[128,256]{1,0:T(8,128)(2,1)S(1)}, u32[]{:S(2)}, u32[]{:S(2)}) collective-permute-start(bf16[128,256]{1,0:T(8,128)(2,1)S(1)} %get-tuple-element.14), channel_id=1, source_target_pairs={{0,1},{1,2},{2,3},{3,4},{4,5},{5,6},{6,7},{8,9},{9,10},{10,11},{11... | collective-permute-start | bytes 196616 | tf_op jit(solution)/shard_map/ppermute | solution.py:22
  10.2 6.2 %collective-permute-start.1 = (bf16[128,256]{1,0:T(8,128)(2,1)S(1)}, bf16[128,256]{1,0:T(8,128)(2,1)S(1)}, u32[]{:S(2)}, u32[]{:S(2)}) collective-permute-start(bf16[128,256]{1,0:T(8,128)(2,1)S(1)} %get-tuple-element.13), channel_id=1, source_target_pairs={{1,0},{2,1},{3,2},{4,3},{5,4},{6,5},{7,6},{9,8},{10,9},{11,10},{12... | collective-permute-start | bytes 196616 | tf_op jit(solution)/shard_map/ppermute | solution.py:25
  14.2 1.7 %copy-start = (bf16[1,1024,256]{2,1,0:T(8,128)(2,1)S(1)}, bf16[1,1024,256]{2,1,0:T(8,128)(2,1)}, u32[]{:S(2)}) copy-start(bf16[1,1024,256]{2,1,0:T(8,128)(2,1)} %param.12) | copy-start | bytes 1572868
  14.9 1.5 %copy-start.3 = (bf16[7,256,256]{2,1,0:T(8,128)(2,1)S(1)}, bf16[7,256,256]{2,1,0:T(8,128)(2,1)}, u32[]{:S(2)}) copy-start(bf16[7,256,256]{2,1,0:T(8,128)(2,1)} %weight_ref.1) | copy-start | bytes 2752516
  14.9 1.5 %copy-start.6 = (f32[256]{0:T(256)S(1)}, f32[256]{0:T(256)}, u32[]{:S(2)}) copy-start(f32[256]{0:T(256)} %param.19) | copy-start | bytes 3076
  14.9 1.5 %copy-start.7 = (f32[256]{0:T(256)S(1)}, f32[256]{0:T(256)}, u32[]{:S(2)}) copy-start(f32[256]{0:T(256)} %param.20) | copy-start | bytes 3076
  14.9 1.5 %copy-start.8 = (f32[256]{0:T(256)S(1)}, f32[256]{0:T(256)}, u32[]{:S(2)}) copy-start(f32[256]{0:T(256)} %param.21) | copy-start | bytes 3076
  16.4 1.0 %copy-start.4 = (bf16[256,768]{1,0:T(8,128)(2,1)S(1)}, bf16[256,768]{1,0:T(8,128)(2,1)}, u32[]{:S(2)}) copy-start(bf16[256,768]{1,0:T(8,128)(2,1)} %qkv_ref.1) | copy-start | bytes 1179652
  31.2 1.0 %copy-start.1 = (f32[1024,256]{1,0:T(8,128)}, f32[1024,256]{1,0:T(8,128)S(1)}, u32[]{:S(2)}) copy-start(f32[1024,256]{1,0:T(8,128)S(1)} %get-tuple-element.10.hidden_ref) | copy-start | bytes 3145732
  33.9 13.2 %copy-start.9 = (s32[1,64]{1,0:T(1,128)S(1)}, s32[1,64]{1,0:T(1,128)}, u32[]{:S(2)}) copy-start(s32[1,64]{1,0:T(1,128)} %param.15) | copy-start | bytes 772
  33.9 13.3 %copy-start.12 = (s32[1024]{0:T(1024)S(1)}, s32[1024]{0:T(1024)}, u32[]{:S(2)}) copy-start(s32[1024]{0:T(1024)} %get-tuple-element.16) | copy-start | bytes 12292
  34.0 34.6 %all-to-all-start = ((bf16[8,128,512]{2,1,0:T(8,128)(2,1)}), bf16[8,128,512]{2,1,0:T(8,128)(2,1)}, u32[]{:S(2)}, u32[]{:S(2)}) async-start(bf16[8,128,512]{2,1,0:T(8,128)(2,1)} %gather_fusion.4), calls=%async_computation | async-start | bytes 2097152 | tf_op jit(solution)/shard_map/all_to_all | solution.py:178
  40.3 28.1 %collective-permute-start.4 = (bf16[128,512]{1,0:T(8,128)(2,1)S(1)}, bf16[128,512]{1,0:T(8,128)(2,1)S(1)}, u32[]{:S(2)}, u32[]{:S(2)}) collective-permute-start(bf16[128,512]{1,0:T(8,128)(2,1)S(1)} %get-tuple-element.11), channel_id=1, source_target_pairs={{0,1},{1,2},{2,3},{3,4},{4,5},{5,6},{6,7},{8,9},{9,10},{10,11},{11... | collective-permute-start | bytes 393224 | tf_op jit(solution)/shard_map/ppermute | solution.py:22
  43.7 24.8 %collective-permute-start.5 = (bf16[128,512]{1,0:T(8,128)(2,1)S(1)}, bf16[128,512]{1,0:T(8,128)(2,1)S(1)}, u32[]{:S(2)}, u32[]{:S(2)}) collective-permute-start(bf16[128,512]{1,0:T(8,128)(2,1)S(1)} %get-tuple-element.12), channel_id=1, source_target_pairs={{1,0},{2,1},{3,2},{4,3},{5,4},{6,5},{7,6},{9,8},{10,9},{11,10},{12... | collective-permute-start | bytes 393224 | tf_op jit(solution)/shard_map/ppermute | solution.py:25
  48.9 19.7 %copy-start.5 = (bf16[256,256]{1,0:T(8,128)(2,1)S(1)}, bf16[256,256]{1,0:T(8,128)(2,1)}, u32[]{:S(2)}) copy-start(bf16[256,256]{1,0:T(8,128)(2,1)} %out_w_ref.1) | copy-start | bytes 393220
  68.6 1.2 %copy-start.2 = (f32[1024,256]{1,0:T(8,128)S(1)}, f32[1024,256]{1,0:T(8,128)}, u32[]{:S(2)}) copy-start(f32[1024,256]{1,0:T(8,128)} %copy-done.1) | copy-start | bytes 3145732

commit v2 on v1

v2 whole, which is shorter than its diff:
```python
import functools
import math

import jax
import jax.numpy as jnp
from jax import lax
from jax.experimental import pallas as pl
from jax.experimental.pallas import tpu as pltpu
from jax.sharding import PartitionSpec as P

D = 256
HEADS = 8
BLK = 128
EDGE = 128
FACE = 256


MESH = pl.DeviceIdType.MESH


def table_kernel(n_space, n_ctx, rows_ref, own_ref, table_ref, face_ref, send_sem, recv_sem):
    space, ctx = lax.axis_index("space"), lax.axis_index("ctx")
    count = own_ref.shape[0]
    base = count + 2 * EDGE
    sides = (
        (ctx < n_ctx - 1, ctx > 0, (space, ctx + 1)),
        (ctx > 0, ctx < n_ctx - 1, (space, ctx - 1)),
        (space < n_space - 1, space > 0, (space + 1, ctx)),
        (space > 0, space < n_space - 1, (space - 1, ctx)),
    )
    barrier = pltpu.get_barrier_semaphore()
    for there, _, peer in sides:
        @pl.when(there)
        def _():
            pl.semaphore_signal(barrier, inc=1, device_id=peer, device_id_type=MESH)
    pl.semaphore_wait(barrier, sum(there.astype(jnp.int32) for there, _, _ in sides))
    targets = (
        (0, EDGE), (EDGE + count, EDGE), (base, FACE), (base + 2 * FACE, FACE)
    )
    sources = (
        own_ref.at[pl.ds(count - EDGE, EDGE)], own_ref.at[pl.ds(0, EDGE)], face_ref, face_ref
    )
    copies = [
        pltpu.make_async_remote_copy(
            src_ref=sources[i],
            dst_ref=table_ref.at[pl.ds(*targets[i])],
            send_sem=send_sem.at[i],
            recv_sem=recv_sem.at[i],
            device_id=sides[i][2],
            device_id_type=MESH,
        )
        for i in range(4)
    ]
    for i in (0, 1):
        pl.when(sides[i][0])(copies[i].start)
    place = lax.broadcasted_iota(jnp.int32, (FACE, count), 1)
    hot = jnp.where(rows_ref[...] == place, 1.0, 0.0).astype(jnp.bfloat16)
    face = jnp.dot(hot, own_ref[...], preferred_element_type=jnp.float32).astype(jnp.bfloat16)
    face_ref[...] = face
    for i in (2, 3):
        pl.when(sides[i][0])(copies[i].start)
    table_ref[EDGE : EDGE + count, :] = own_ref[...]
    table_ref[base + FACE : base + 2 * FACE, :] = face
    for i in range(4):
        first, width = targets[i]

        @pl.when(jnp.logical_not(sides[i][1]))
        def _():
            table_ref[first : first + width, :] = jnp.zeros((width, D), jnp.bfloat16)
    for i in range(4):
        pl.when(sides[i][0])(copies[i].wait_send)
        pl.when(sides[i][1])(copies[i].wait_recv)


def build_table(rows, own, n_space, n_ctx):
    count, width = own.shape
    vmem = pl.BlockSpec(memory_space=pltpu.VMEM)
    return pl.pallas_call(
        functools.partial(table_kernel, n_space, n_ctx),
        in_specs=[vmem, vmem],
        out_specs=vmem,
        out_shape=jax.ShapeDtypeStruct((count + 2 * EDGE + 3 * FACE, width), own.dtype),
        scratch_shapes=[
            pltpu.VMEM((FACE, width), own.dtype),
            pltpu.SemaphoreType.DMA((4,)),
            pltpu.SemaphoreType.DMA((4,)),
        ],
        compiler_params=pltpu.CompilerParams(
            collective_id=0, has_side_effects=True, vmem_limit_bytes=24 * 2**20
        ),
    )(rows[:, None], own)


def exchange_kernel(n_ctx, out_ref, ends_ref, far_ref, send_sem, recv_sem, local_sem):
    space, ctx = lax.axis_index("space"), lax.axis_index("ctx")
    barrier = pltpu.get_barrier_semaphore()
    for step in range(1, n_ctx):
        peer = lax.rem(ctx + step, n_ctx)
        pl.semaphore_signal(barrier, inc=1, device_id=(space, peer), device_id_type=MESH)
    pl.semaphore_wait(barrier, n_ctx - 1)
    copies = []
    for step in range(1, n_ctx):
        peer = lax.rem(ctx + step, n_ctx)
        copies.append(
            pltpu.make_async_remote_copy(
                src_ref=out_ref.at[peer],
                dst_ref=far_ref.at[ctx],
                send_sem=send_sem.at[step],
                recv_sem=recv_sem.at[step],
                device_id=(space, peer),
                device_id_type=MESH,
            )
        )
    sides = (
        (ctx < n_ctx - 1, ctx > 0, ctx + 1, 1, n_ctx),
        (ctx > 0, ctx < n_ctx - 1, ctx - 1, 0, n_ctx + 1),
    )
    edges = [
        pltpu.make_async_remote_copy(
            src_ref=ends_ref.at[source],
            dst_ref=far_ref.at[slot],
            send_sem=send_sem.at[slot],
            recv_sem=recv_sem.at[slot],
            device_id=(space, peer),
            device_id_type=MESH,
        )
        for _, _, peer, source, slot in sides
    ]
    order = sorted(range(1, n_ctx), key=lambda step: abs(step - n_ctx // 2))
    for step in order:
        copies[step - 1].start()
    for side, edge in zip(sides, edges):
        pl.when(side[0])(edge.start)
    own = pltpu.make_async_copy(out_ref.at[ctx], far_ref.at[ctx], local_sem)
    own.start()
    for side in sides:
        @pl.when(jnp.logical_not(side[1]))
        def _():
            far_ref[side[4]] = jnp.zeros(far_ref.shape[1:], jnp.bfloat16)
    own.wait()
    for copy in copies:
        copy.wait()
    for side, edge in zip(sides, edges):
        pl.when(side[0])(edge.wait_send)
        pl.when(side[1])(edge.wait_recv)


def exchange(outgoing, ends, n_ctx):
    vmem = pl.BlockSpec(memory_space=pltpu.VMEM)
    return pl.pallas_call(
        functools.partial(exchange_kernel, n_ctx),
        in_specs=[vmem, vmem],
        out_specs=vmem,
        out_shape=jax.ShapeDtypeStruct((n_ctx + 2,) + outgoing.shape[1:], outgoing.dtype),
        scratch_shapes=[
            pltpu.SemaphoreType.DMA((n_ctx + 2,)),
            pltpu.SemaphoreType.DMA((n_ctx + 2,)),
            pltpu.SemaphoreType.DMA,
        ],
        compiler_params=pltpu.CompilerParams(
            collective_id=1, has_side_effects=True, vmem_limit_bytes=24 * 2**20
        ),
    )(outgoing, ends)


ROWS = 256


def encode_kernel(
    pick_ref, ids_ref, own_ref, table_ref, weight_ref, bias_ref, gain_ref, shift_ref, qkv_ref,
    hidden_ref, query_ref, kv_ref, outgoing_ref, ends_ref, normed_ref,
):
    rows = own_ref.shape[0]
    count = table_ref.shape[0]
    own = own_ref[...]
    conv = jnp.dot(own, weight_ref[0], preferred_element_type=jnp.float32)
    lane = lax.broadcasted_iota(jnp.int32, (rows, 128), 1)
    ids = ids_ref[...]
    for offset in range(6):
        column = jnp.broadcast_to(ids[:, offset : offset + 1], (rows, 128))
        low = column & 127
        high = (column >> 7).astype(jnp.float32).astype(jnp.bfloat16)
        hot = jnp.where(low == lane, 1.0, 0.0).astype(jnp.bfloat16)
        zero = jnp.zeros_like(hot)
        chosen = jnp.concatenate(
            [jnp.where(high == jnp.bfloat16(part), hot, zero) for part in range(count // 128)], 1
        )
        picked = jnp.dot(chosen, table_ref[...], preferred_element_type=jnp.float32)
        conv = conv + jnp.dot(
            picked.astype(jnp.bfloat16), weight_ref[offset + 1], preferred_element_type=jnp.float32
        )
    hidden = own.astype(jnp.float32) + conv + bias_ref[...]
    hidden_ref[...] = hidden
    center = hidden - jnp.mean(hidden, axis=-1, keepdims=True)
    variance = jnp.mean(center * center, axis=-1, keepdims=True)
    normed = (center * lax.rsqrt(variance + 1e-05) * gain_ref[...] + shift_ref[...]).astype(jnp.bfloat16)
    projected = jnp.dot(normed, qkv_ref[...], preferred_element_type=jnp.float32).astype(jnp.bfloat16)
    query_ref[...] = projected[:, :D]
    kv_ref[...] = projected[:, D:]
    step = pl.program_id(0)
    normed_ref[pl.ds(pl.multiple_of(step * rows, rows), rows), :] = normed

    @pl.when(step == pl.num_programs(0) - 1)
    def _():
        ends_ref[0] = normed_ref[:BLK, :]
        ends_ref[1] = normed_ref[normed_ref.shape[0] - BLK :, :]
        for peer in range(outgoing_ref.shape[0]):
            first = pl.multiple_of(pick_ref[lax.axis_index("ctx"), peer] * BLK, BLK)
            outgoing_ref[peer] = normed_ref[pl.ds(first, BLK), :]


def encode(pick, ids, own, table, weight, bias, gain, shift, w_qkv):
    count, width = own.shape
    whole = lambda shape: pl.BlockSpec(shape, lambda i, *_: (0,) * len(shape))
    tile = lambda cols: pl.BlockSpec((ROWS, cols), lambda i, *_: (i, 0))
    peers = pick.shape[0]
    return pl.pallas_call(
        encode_kernel,
        grid_spec=pltpu.PrefetchScalarGridSpec(
            num_scalar_prefetch=1,
            grid=(count // ROWS,),
            in_specs=[
                tile(6), tile(width), whole(table.shape), whole(weight.shape),
                whole((1, width)), whole((1, width)), whole((1, width)), whole(w_qkv.shape),
            ],
            out_specs=[
                tile(width), tile(width), tile(2 * width),
                whole((peers, BLK, width)), whole((2, BLK, width)),
            ],
            scratch_shapes=[pltpu.VMEM((count, width), jnp.bfloat16)],
        ),
        out_shape=[
            jax.ShapeDtypeStruct((count, width), jnp.float32),
            jax.ShapeDtypeStruct((count, width), jnp.bfloat16),
            jax.ShapeDtypeStruct((count, 2 * width), jnp.bfloat16),
            jax.ShapeDtypeStruct((peers, BLK, width), jnp.bfloat16),
            jax.ShapeDtypeStruct((2, BLK, width), jnp.bfloat16),
        ],
        compiler_params=pltpu.CompilerParams(vmem_limit_bytes=40 * 2**20),
    )(pick, ids, own, table, weight, bias[None], gain[None], shift[None], w_qkv)


GROUP = 4


def attend_kernel(
    slots_ref, lens_ref, pick_ref, query_ref, near_ref, far_ref, qkv_ref, hidden_ref, out_w_ref,
    out_ref, far_kv_ref, window_ref, kv_ref,
):
    blk = pl.program_id(0)
    peers = pick_ref.shape[0]
    count = near_ref.shape[0]
    blocks = count // BLK
    ctx = lax.axis_index("ctx")

    @pl.when(blk == 0)
    def _():
        kv_weight = qkv_ref[:, D:]
        for peer in range(peers):
            far_kv_ref[peer * BLK : (peer + 1) * BLK, :] = jnp.dot(
                far_ref[peer], kv_weight, preferred_element_type=jnp.float32
            ).astype(jnp.bfloat16)
        window_ref[BLK : BLK + count, :] = near_ref[...]
        for side, first in ((peers, 0), (peers + 1, BLK + count)):
            window_ref[first : first + BLK, :] = jnp.dot(
                far_ref[side], kv_weight, preferred_element_type=jnp.float32
            ).astype(jnp.bfloat16)

    start = pl.multiple_of(blk * BLK, BLK)
    kv_ref[0 : 3 * BLK, :] = window_ref[pl.ds(start, 3 * BLK), :]
    lens = []
    for part in range(3):
        block = ctx * blocks + blk + part - 1
        inside = jnp.logical_and(block >= 0, block < peers * blocks)
        lens.append(jnp.where(inside, lens_ref[jnp.clip(block, 0, peers * blocks - 1)], 0))
    for slot in range(4):
        source = slots_ref[blk, slot]
        lens.append(lens_ref[source * blocks + pick_ref[source, ctx]])
        where = pl.multiple_of(source * BLK, BLK)
        kv_ref[(3 + slot) * BLK : (4 + slot) * BLK, :] = far_kv_ref[pl.ds(where, BLK), :]
    lane = lax.broadcasted_iota(jnp.int32, (1, BLK), 1)
    mask = jnp.concatenate([jnp.where(lane < valid, 0.0, -1e30) for valid in lens], 1)
    head_dim = D // HEADS
    head_of = lax.broadcasted_iota(jnp.int32, (BLK, D), 1) // head_dim
    query = query_ref[...]
    keys = kv_ref[:, :D]
    values = kv_ref[:, D:]
    scale = 1.0 / math.sqrt(head_dim)
    attended = jnp.zeros((BLK, D), jnp.float32)
    for group in range(0, HEADS, GROUP):
        stacked = jnp.concatenate(
            [jnp.where(head_of == head, query, jnp.zeros_like(query)) for head in range(group, group + GROUP)], 0
        )
        scores = lax.dot_general(
            stacked, keys, (((1,), (1,)), ((), ())), preferred_element_type=jnp.float32
        ) * scale + mask
        raw = jnp.exp(scores - jnp.max(scores, axis=-1, keepdims=True))
        inverse = 1.0 / jnp.sum(raw, axis=-1, keepdims=True)
        weights = (raw * inverse).astype(jnp.bfloat16)
        mixed = jnp.dot(weights, values, preferred_element_type=jnp.float32)
        for part in range(GROUP):
            attended = jnp.where(head_of == group + part, mixed[part * BLK : (part + 1) * BLK], attended)
    out = hidden_ref[...] + jnp.dot(
        attended.astype(jnp.bfloat16), out_w_ref[...], preferred_element_type=jnp.float32
    )
    out_ref[...] = out.astype(jnp.bfloat16)


def attend(slots, lens, pick, queries, near, far, w_qkv, hidden, w_out):
    count, width = queries.shape
    whole = lambda shape: pl.BlockSpec(shape, lambda i, *_: (0,) * len(shape))
    tile = pl.BlockSpec((BLK, width), lambda i, *_: (i, 0))
    return pl.pallas_call(
        attend_kernel,
        grid_spec=pltpu.PrefetchScalarGridSpec(
            num_scalar_prefetch=3,
            grid=(count // BLK,),
            in_specs=[
                tile, whole(near.shape), whole(far.shape), whole(w_qkv.shape), tile, whole(w_out.shape)
            ],
            out_specs=tile,
            scratch_shapes=[
                pltpu.VMEM((pick.shape[0] * BLK, 2 * width), jnp.bfloat16),
                pltpu.VMEM((count + 2 * BLK, 2 * width), jnp.bfloat16),
                pltpu.VMEM((7 * BLK, 2 * width), jnp.bfloat16),
            ],
        ),
        out_shape=jax.ShapeDtypeStruct((count, width), jnp.bfloat16),
        compiler_params=pltpu.CompilerParams(vmem_limit_bytes=48 * 2**20),
    )(slots, lens, pick, queries, near, far, w_qkv, hidden, w_out)


def on_device(
    feats,
    face_rows,
    neighbours,
    block_len,
    dilated,
    pick,
    cpe_weight,
    cpe_bias,
    ln_gain,
    ln_bias,
    w_qkv,
    w_out,
):
    voxels = feats[0]
    n_space, n_ctx = lax.axis_size("space"), lax.axis_size("ctx")
    table = build_table(face_rows[0], voxels, n_space, n_ctx)
    hidden, queries, near, outgoing, ends = encode(
        pick[0], neighbours[0], voxels, table, cpe_weight, cpe_bias, ln_gain, ln_bias, w_qkv
    )
    far = exchange(outgoing, ends, n_ctx)
    return attend(dilated[0], block_len[0], pick[0], queries, near, far, w_qkv, hidden, w_out)[None]


def solution(mesh):
    placed = (
        P("space", "ctx", None),
        P("space", "ctx"),
        P("space", "ctx", None),
        P("space", None),
        P("space", "ctx", None),
        P("space", None, None),
        P(),
        P(),
        P(),
        P(),
        P(),
        P(),
    )
    return jax.shard_map(
        on_device, mesh=mesh, in_specs=placed, out_specs=P("space", "ctx", None), check_vma=False
    )
```

time: 94.9 us -> 69.3 us (0.73)
  Pallas kernels: 38 us -> 61.4 us
  starting transfers between devices: 22.7 us -> 0 us
  waiting for transfers between devices: 20 us -> 0 us
  local copies, waits for them, and re-layouts: 11.4 us -> 7.46 us
  other arithmetic: 1.61 us -> 0 us
    pallas_call x1 -> x3, Pallas kernels: 13.8 us -> 38.1 us  [the longest x1 16.9 us: exchange(): pl.pallas_call(functools.partial(exchange_kernel, n_ctx), in_specs=[vmem,...]
    ppermute x6 -> x0, waiting for transfers between devices: 20 us -> none  [the longest x3 19.6 us: extended(): lax.ppermute(lax.slice_in_dim(block, block.shape[dim] - width, None, axis...]
    ppermute x6 -> x0, starting transfers between devices: 16.5 us -> none  [the longest x3 8.52 us: extended(): lax.ppermute(lax.slice_in_dim(block, block.shape[dim] - width, None, axis...]
    gather x9 -> x0, local copies, waits for them, and re-layouts: 6.21 us -> none  [the longest x1 2.07 us: on_device(): face_out = voxels[face_rows[0]]]
    all_to_all x1 -> x0, starting transfers between devices: 6.21 us -> none  [on_device(): lax.all_to_all(outgoing, 'ctx', split_axis=0, concat_axis=0, tiled=True)]
    unnamed x34 -> x35, local copies, waits for them, and re-layouts: 3.54 us -> 7.24 us
  transfers between devices with their start and end apart: 7 -> 0, of which waited for: 2 -> 0; matrix products, arithmetic and copies ran while one was open for 6% -> 0% of each run, Pallas kernels for 0% -> 0%
where the time goes in v2:
time: 69.3 us; the launch traced here: 69 us
  Pallas kernels  61.4 us (89%)
  local copies, waits for them, and re-layouts  7.46 us (11%)
    pallas_call x1, Pallas kernels, attend(): pl.pallas_call(attend_kernel, grid_spec=pltpu.PrefetchScalarGridSpec(num_...  23.3 us
    pallas_call x1, Pallas kernels, exchange(): pl.pallas_call(functools.partial(exchange_kernel, n_ctx), in_specs=[vmem,...  16.9 us
    pallas_call x1, Pallas kernels, encode(): pl.pallas_call(encode_kernel, grid_spec=pltpu.PrefetchScalarGridSpec(num_...  14.4 us
    unnamed x35, local copies, waits for them, and re-layouts  7.24 us
    pallas_call x1, Pallas kernels, build_table(): pl.pallas_call(functools.partial(table_kernel, n_space, n_ctx), in_specs=...  6.74 us

profile of v2, /device:TPU:16, one launch (start us, length us, event | category | flops | bytes accessed | tf_op | source)
XLA Modules:
  0.0 69.0 jit_solution(10746071317476413886)
XLA Ops:
  0.0 0.7 copy-done.16
  0.7 0.1 copy.16.rows_ref
  0.8 0.0 copy-start
  0.8 1.0 %copy-done = bf16[1,1024,256]{2,1,0:T(8,128)(2,1)S(1)} copy-done((bf16[1,1024,256]{2,1,0:T(8,128)(2,1)S(1)}, bf16[1,1024,256]{2,1,0:T(8,128)(2,1)}, u32[]{:S(2)}) %copy-start) | copy-done | bytes 524312
  1.9 6.7 %shard_map.118.table_ref = bf16[2048,256]{1,0:T(8,128)(2,1)S(1)} custom-call(s32[256,1]{1,0:T(8,128)S(1)} %copy.16.rows_ref, bf16[1024,256]{1,0:T(8,128)(2,1)S(1)} %bitcast.10), custom_call_target="tpu_custom_call" | custom-call | tf_op jit(solution)/shard_map/pallas_call | solution.py:78
  8.6 0.0 copy-start.1
  8.6 0.0 copy-start.11
  8.7 0.0 copy-start.12
  8.7 0.2 copy.15
  8.9 0.0 copy-start.9
  8.9 0.0 copy-start.10
  8.9 0.7 %copy-done.1 = bf16[1,1024,256]{2,1,0:T(8,128)(2,1)S(1)} copy-done((bf16[1,1024,256]{2,1,0:T(8,128)(2,1)S(1)}, bf16[1,1024,256]{2,1,0:T(8,128)(2,1)}, u32[]{:S(2)}) %copy-start.1) | copy-done | bytes 524312
  9.7 0.0 copy-done.12
  9.7 0.0 copy-start.5
  9.7 1.2 %copy-done.5 = bf16[7,256,256]{2,1,0:T(8,128)(2,1)S(1)} copy-done((bf16[7,256,256]{2,1,0:T(8,128)(2,1)S(1)}, bf16[7,256,256]{2,1,0:T(8,128)(2,1)}, u32[]{:S(2)}) %copy-start.5) | copy-done | bytes 917528
  10.9 14.4 %shard_map.119 = (f32[1024,256]{1,0:T(8,128)S(1)}, bf16[1024,256]{1,0:T(8,128)(2,1)S(1)}, bf16[1024,512]{1,0:T(8,128)(2,1)S(1)}, bf16[8,128,256]{2,1,0:T(8,128)(2,1)S(1)}, bf16[2,128,256]{2,1,0:T(8,128)(2,1)S(1)}) custom-call(s32[8,8]{1,0:T(8,128)S(1)} %bitcast.13, s32[1024,6]{1,0:T(8,128)S(1)} %bitcast.12, bf16[1024,256]{1,0:T(8,128)(2,1)S(1)} %bitcast.11, ...), custom_call_target="tpu_custom_call" | custom-call | tf_op jit(solution)/shard_map/pallas_call | solution.py:217
  25.3 1.0 %copy-done.3 = bf16[1024,512]{1,0:T(8,128)(2,1)} copy-done((bf16[1024,512]{1,0:T(8,128)(2,1)}, bf16[1024,512]{1,0:T(8,128)(2,1)S(1)}, u32[]{:S(2)}) %copy-start.3) | copy-done | bytes 1048600
  26.3 16.9 %shard_map.120.far_ref = bf16[10,128,256]{2,1,0:T(8,128)(2,1)S(1)} custom-call(bf16[8,128,256]{2,1,0:T(8,128)(2,1)S(1)} %get-tuple-element.12.out_ref, bf16[2,128,256]{2,1,0:T(8,128)(2,1)S(1)} %get-tuple-element.13.ends_ref), custom_call_target="tpu_custom_call" | custom-call | tf_op jit(solution)/shard_map/pallas_call | solution.py:150
  43.2 0.0 copy-start.15
  43.2 0.7 copy-done.15
  43.9 0.1 copy.17.slots_ref
  44.0 0.6 copy-done.13
  44.7 1.0 %copy-done.7 = bf16[1024,256]{1,0:T(8,128)(2,1)S(1)} copy-done((bf16[1024,256]{1,0:T(8,128)(2,1)S(1)}, bf16[1024,256]{1,0:T(8,128)(2,1)}, u32[]{:S(2)}) %copy-start.7) | copy-done | bytes 524312
  45.7 23.3 %shard_map.121 = bf16[1024,256]{1,0:T(8,128)(2,1)} custom-call(s32[8,4]{1,0:T(8,128)S(1)} %copy.17.slots_ref, s32[64]{0:T(128)S(1)} %bitcast.18, s32[8,8]{1,0:T(8,128)S(1)} %bitcast.14, bf16[1024,256]{1,0:T(8,128)(2,1)S(1)} %copy-done.7, bf16[1024,512]{1,0:T(8,128)(2,1)S(1)} %copy-done.4, bf16[10,128,256]{2,1,0:T(8,128)(2,1)S(1)} %shard_map.120.far_ref, ...), custom_call_target="tpu_custom_call" | custom-call | tf_op jit(solution)/shard_map/pallas_call | solution.py:313
  (17 shorter events, 0.0 us)
Async XLA Ops:
  0.0 0.7 copy-start.16
  0.8 1.0 %copy-start = (bf16[1,1024,256]{2,1,0:T(8,128)(2,1)S(1)}, bf16[1,1024,256]{2,1,0:T(8,128)(2,1)}, u32[]{:S(2)}) copy-start(bf16[1,1024,256]{2,1,0:T(8,128)(2,1)} %param.12) | copy-start | bytes 1572868
  1.9 6.8 %copy-start.14 = (s32[1,1024,6]{1,0,2:T(1,128)S(1)}, s32[1,1024,6]{1,0,2:T(1,128)}, u32[]{:S(2)}) copy-start(s32[1,1024,6]{1,0,2:T(1,128)} %param.14) | copy-start | bytes 73732
  1.9 7.1 %copy-start.2 = (bf16[256,768]{1,0:T(8,128)(2,1)S(1)}, bf16[256,768]{1,0:T(8,128)(2,1)}, u32[]{:S(2)}) copy-start(bf16[256,768]{1,0:T(8,128)(2,1)} %qkv_ref.3) | copy-start | bytes 1179652
  8.6 1.0 %copy-start.1 = (bf16[1,1024,256]{2,1,0:T(8,128)(2,1)S(1)}, bf16[1,1024,256]{2,1,0:T(8,128)(2,1)}, u32[]{:S(2)}) copy-start(bf16[1,1024,256]{2,1,0:T(8,128)(2,1)} %param.12) | copy-start | bytes 1572868
  8.6 1.0 %copy-start.11 = (f32[256]{0:T(256)S(1)}, f32[256]{0:T(256)}, u32[]{:S(2)}) copy-start(f32[256]{0:T(256)} %param.20) | copy-start | bytes 3076
  8.7 1.0 %copy-start.12 = (f32[256]{0:T(256)S(1)}, f32[256]{0:T(256)}, u32[]{:S(2)}) copy-start(f32[256]{0:T(256)} %param.21) | copy-start | bytes 3076
  8.9 0.8 %copy-start.9 = (s32[1,8,8]{2,1,0:T(8,128)S(1)}, s32[1,8,8]{2,1,0:T(8,128)}, u32[]{:S(2)}) copy-start(s32[1,8,8]{2,1,0:T(8,128)} %param.17) | copy-start | bytes 772
  8.9 0.8 %copy-start.10 = (f32[256]{0:T(256)S(1)}, f32[256]{0:T(256)}, u32[]{:S(2)}) copy-start(f32[256]{0:T(256)} %param.19) | copy-start | bytes 3076
  9.7 1.2 %copy-start.5 = (bf16[7,256,256]{2,1,0:T(8,128)(2,1)S(1)}, bf16[7,256,256]{2,1,0:T(8,128)(2,1)}, u32[]{:S(2)}) copy-start(bf16[7,256,256]{2,1,0:T(8,128)(2,1)} %weight_ref.1) | copy-start | bytes 2752516
  25.3 1.0 %copy-start.3 = (bf16[1024,512]{1,0:T(8,128)(2,1)}, bf16[1024,512]{1,0:T(8,128)(2,1)S(1)}, u32[]{:S(2)}) copy-start(bf16[1024,512]{1,0:T(8,128)(2,1)S(1)} %get-tuple-element.11.near_ref) | copy-start | bytes 3145732
  26.3 16.9 %copy-start.6 = (bf16[1024,256]{1,0:T(8,128)(2,1)}, bf16[1024,256]{1,0:T(8,128)(2,1)S(1)}, u32[]{:S(2)}) copy-start(bf16[1024,256]{1,0:T(8,128)(2,1)S(1)} %get-tuple-element.10.query_ref) | copy-start | bytes 1572868
  26.3 17.7 %copy-start.4 = (bf16[1024,512]{1,0:T(8,128)(2,1)S(1)}, bf16[1024,512]{1,0:T(8,128)(2,1)}, u32[]{:S(2)}) copy-start(bf16[1024,512]{1,0:T(8,128)(2,1)} %copy-done.3) | copy-start | bytes 3145732
  26.3 17.7 %copy-start.8 = (bf16[256,256]{1,0:T(8,128)(2,1)S(1)}, bf16[256,256]{1,0:T(8,128)(2,1)}, u32[]{:S(2)}) copy-start(bf16[256,256]{1,0:T(8,128)(2,1)} %out_w_ref.1) | copy-start | bytes 393220
  43.2 0.7 copy-start.15
  44.0 0.7 copy-start.13
  44.7 1.0 %copy-start.7 = (bf16[1024,256]{1,0:T(8,128)(2,1)S(1)}, bf16[1024,256]{1,0:T(8,128)(2,1)}, u32[]{:S(2)}) copy-start(bf16[1024,256]{1,0:T(8,128)(2,1)} %copy-done.6) | copy-start | bytes 1572868

commit v3 on v2

--- a/solution.py
+++ b/solution.py
@@ -86,7 +86,7 @@
             pltpu.SemaphoreType.DMA((4,)),
         ],
         compiler_params=pltpu.CompilerParams(
-            collective_id=0, has_side_effects=True, vmem_limit_bytes=24 * 2**20
+            collective_id=0, has_side_effects=True, vmem_limit_bytes=8 * 2**20
         ),
     )(rows[:, None], own)
 
@@ -158,7 +158,7 @@
             pltpu.SemaphoreType.DMA,
         ],
         compiler_params=pltpu.CompilerParams(
-            collective_id=1, has_side_effects=True, vmem_limit_bytes=24 * 2**20
+            collective_id=1, has_side_effects=True, vmem_limit_bytes=8 * 2**20
         ),
     )(outgoing, ends)
 
@@ -167,12 +167,13 @@
 
 
 def encode_kernel(
-    pick_ref, ids_ref, own_ref, table_ref, weight_ref, bias_ref, gain_ref, shift_ref, qkv_ref,
+    pick_ref, ids_ref, table_ref, weight_ref, bias_ref, gain_ref, shift_ref, qkv_ref,
     hidden_ref, query_ref, kv_ref, outgoing_ref, ends_ref, normed_ref,
 ):
-    rows = own_ref.shape[0]
+    rows = ids_ref.shape[0]
     count = table_ref.shape[0]
-    own = own_ref[...]
+    step = pl.program_id(0)
+    own = table_ref[pl.ds(pl.multiple_of(EDGE + step * rows, EDGE), rows), :]
     conv = jnp.dot(own, weight_ref[0], preferred_element_type=jnp.float32)
     lane = lax.broadcasted_iota(jnp.int32, (rows, 128), 1)
     ids = ids_ref[...]
@@ -197,7 +198,6 @@
     projected = jnp.dot(normed, qkv_ref[...], preferred_element_type=jnp.float32).astype(jnp.bfloat16)
     query_ref[...] = projected[:, :D]
     kv_ref[...] = projected[:, D:]
-    step = pl.program_id(0)
     normed_ref[pl.ds(pl.multiple_of(step * rows, rows), rows), :] = normed
 
     @pl.when(step == pl.num_programs(0) - 1)
@@ -209,8 +209,8 @@
             outgoing_ref[peer] = normed_ref[pl.ds(first, BLK), :]
 
 
-def encode(pick, ids, own, table, weight, bias, gain, shift, w_qkv):
-    count, width = own.shape
+def encode(pick, ids, table, weight, bias, gain, shift, w_qkv):
+    count, width = ids.shape[0], table.shape[1]
     whole = lambda shape: pl.BlockSpec(shape, lambda i, *_: (0,) * len(shape))
     tile = lambda cols: pl.BlockSpec((ROWS, cols), lambda i, *_: (i, 0))
     peers = pick.shape[0]
@@ -220,7 +220,7 @@
             num_scalar_prefetch=1,
             grid=(count // ROWS,),
             in_specs=[
-                tile(6), tile(width), whole(table.shape), whole(weight.shape),
+                tile(6), whole(table.shape), whole(weight.shape),
                 whole((1, width)), whole((1, width)), whole((1, width)), whole(w_qkv.shape),
             ],
             out_specs=[
@@ -236,16 +236,16 @@
             jax.ShapeDtypeStruct((peers, BLK, width), jnp.bfloat16),
             jax.ShapeDtypeStruct((2, BLK, width), jnp.bfloat16),
         ],
-        compiler_params=pltpu.CompilerParams(vmem_limit_bytes=40 * 2**20),
-    )(pick, ids, own, table, weight, bias[None], gain[None], shift[None], w_qkv)
-
-
-GROUP = 4
+        compiler_params=pltpu.CompilerParams(vmem_limit_bytes=20 * 2**20),
+    )(pick, ids, table, weight, bias[None], gain[None], shift[None], w_qkv)
+
+
+HALF = 128
 
 
 def attend_kernel(
     slots_ref, lens_ref, pick_ref, query_ref, near_ref, far_ref, qkv_ref, hidden_ref, out_w_ref,
-    out_ref, far_kv_ref, window_ref, kv_ref,
+    out_ref, far_kv_ref, window_ref, keys_ref, values_ref,
 ):
     blk = pl.program_id(0)
     peers = pick_ref.shape[0]
@@ -266,40 +266,55 @@
                 far_ref[side], kv_weight, preferred_element_type=jnp.float32
             ).astype(jnp.bfloat16)
 
-    start = pl.multiple_of(blk * BLK, BLK)
-    kv_ref[0 : 3 * BLK, :] = window_ref[pl.ds(start, 3 * BLK), :]
-    lens = []
-    for part in range(3):
-        block = ctx * blocks + blk + part - 1
-        inside = jnp.logical_and(block >= 0, block < peers * blocks)
-        lens.append(jnp.where(inside, lens_ref[jnp.clip(block, 0, peers * blocks - 1)], 0))
-    for slot in range(4):
-        source = slots_ref[blk, slot]
-        lens.append(lens_ref[source * blocks + pick_ref[source, ctx]])
-        where = pl.multiple_of(source * BLK, BLK)
-        kv_ref[(3 + slot) * BLK : (4 + slot) * BLK, :] = far_kv_ref[pl.ds(where, BLK), :]
-    lane = lax.broadcasted_iota(jnp.int32, (1, BLK), 1)
-    mask = jnp.concatenate([jnp.where(lane < valid, 0.0, -1e30) for valid in lens], 1)
+        values_ref[:, :, HALF:] = jnp.ones((D // HALF, 7 * BLK, HALF), jnp.bfloat16)
+
+    row = lax.broadcasted_iota(jnp.int32, (BLK, HALF), 0)
+    lane = lax.broadcasted_iota(jnp.int32, (BLK, HALF), 1)
+    for part in range(7):
+        if part < 3:
+            block = ctx * blocks + blk + part - 1
+            inside = jnp.logical_and(block >= 0, block < peers * blocks)
+            valid = jnp.where(inside, lens_ref[jnp.clip(block, 0, peers * blocks - 1)], 0)
+            source = window_ref.at[pl.ds(pl.multiple_of((blk + part) * BLK, BLK), BLK)]
+        else:
+            slot = slots_ref[blk, part - 3]
+            valid = lens_ref[slot * blocks + pick_ref[slot, ctx]]
+            source = far_kv_ref.at[pl.ds(pl.multiple_of(slot * BLK, BLK), BLK)]
+        masked = jnp.where(jnp.logical_and(row >= valid, lane == 0), -1e30, 0.0).astype(jnp.bfloat16)
+        first = part * BLK
+        for group in range(D // HALF):
+            keys_ref[group, first : first + BLK, :HALF] = source[:, group * HALF : (group + 1) * HALF]
+            keys_ref[group, first : first + BLK, HALF:] = masked
+            values_ref[group, first : first + BLK, :HALF] = source[
+                :, D + group * HALF : D + (group + 1) * HALF
+            ]
     head_dim = D // HEADS
-    head_of = lax.broadcasted_iota(jnp.int32, (BLK, D), 1) // head_dim
-    query = query_ref[...]
-    keys = kv_ref[:, :D]
-    values = kv_ref[:, D:]
-    scale = 1.0 / math.sqrt(head_dim)
-    attended = jnp.zeros((BLK, D), jnp.float32)
-    for group in range(0, HEADS, GROUP):
+    head_of = lane // head_dim
+    heads = HALF // head_dim
+    adds_mask = jnp.where(lane == 0, 1.0, 0.0).astype(jnp.bfloat16)
+    scale = math.log2(math.e) / math.sqrt(head_dim)
+    halves = []
+    for group in range(D // HALF):
+        query = query_ref[:, group * HALF : (group + 1) * HALF]
         stacked = jnp.concatenate(
-            [jnp.where(head_of == head, query, jnp.zeros_like(query)) for head in range(group, group + GROUP)], 0
+            [
+                jnp.concatenate([jnp.where(head_of == head, query, jnp.zeros_like(query)), adds_mask], 1)
+                for head in range(heads)
+            ],
+            0,
         )
         scores = lax.dot_general(
-            stacked, keys, (((1,), (1,)), ((), ())), preferred_element_type=jnp.float32
-        ) * scale + mask
-        raw = jnp.exp(scores - jnp.max(scores, axis=-1, keepdims=True))
-        inverse = 1.0 / jnp.sum(raw, axis=-1, keepdims=True)
-        weights = (raw * inverse).astype(jnp.bfloat16)
-        mixed = jnp.dot(weights, values, preferred_element_type=jnp.float32)
-        for part in range(GROUP):
-            attended = jnp.where(head_of == group + part, mixed[part * BLK : (part + 1) * BLK], attended)
+            stacked, keys_ref[group], (((1,), (1,)), ((), ())), preferred_element_type=jnp.float32
+        )
+        peak = jnp.max(scores, axis=-1, keepdims=True)
+        weights = jnp.exp2((scores - peak) * scale).astype(jnp.bfloat16)
+        mixed = jnp.dot(weights, values_ref[group], preferred_element_type=jnp.float32)
+        mixed = mixed[:, :HALF] / mixed[:, HALF:]
+        half = mixed[:BLK]
+        for head in range(1, heads):
+            half = jnp.where(head_of == head, mixed[head * BLK : (head + 1) * BLK], half)
+        halves.append(half)
+    attended = jnp.concatenate(halves, 1)
     out = hidden_ref[...] + jnp.dot(
         attended.astype(jnp.bfloat16), out_w_ref[...], preferred_element_type=jnp.float32
     )
@@ -322,11 +337,12 @@
             scratch_shapes=[
                 pltpu.VMEM((pick.shape[0] * BLK, 2 * width), jnp.bfloat16),
                 pltpu.VMEM((count + 2 * BLK, 2 * width), jnp.bfloat16),
-                pltpu.VMEM((7 * BLK, 2 * width), jnp.bfloat16),
+                pltpu.VMEM((width // HALF, 7 * BLK, 2 * HALF), jnp.bfloat16),
+                pltpu.VMEM((width // HALF, 7 * BLK, 2 * HALF), jnp.bfloat16),
             ],
         ),
         out_shape=jax.ShapeDtypeStruct((count, width), jnp.bfloat16),
-        compiler_params=pltpu.CompilerParams(vmem_limit_bytes=48 * 2**20),
+        compiler_params=pltpu.CompilerParams(vmem_limit_bytes=32 * 2**20),
     )(slots, lens, pick, queries, near, far, w_qkv, hidden, w_out)
 
 
@@ -348,7 +364,7 @@
     n_space, n_ctx = lax.axis_size("space"), lax.axis_size("ctx")
     table = build_table(face_rows[0], voxels, n_space, n_ctx)
     hidden, queries, near, outgoing, ends = encode(
-        pick[0], neighbours[0], voxels, table, cpe_weight, cpe_bias, ln_gain, ln_bias, w_qkv
+        pick[0], neighbours[0], table, cpe_weight, cpe_bias, ln_gain, ln_bias, w_qkv
     )
     far = exchange(outgoing, ends, n_ctx)
     return attend(dilated[0], block_len[0], pick[0], queries, near, far, w_qkv, hidden, w_out)[None]

time: 69.3 us -> 66.7 us (0.962)
  Pallas kernels: 61.4 us -> 58.7 us
    pallas_call x1, Pallas kernels: 23.3 us -> 20.6 us  [attend(): pl.pallas_call(attend_kernel, grid_spec=pltpu.PrefetchScalarGridSpec(num_...]
    unnamed x35 -> x29, local copies, waits for them, and re-layouts: 7.24 us -> 7.39 us
where the time goes in v3:
time: 66.7 us; the launch traced here: 66.4 us
  Pallas kernels  58.7 us (88%)
  local copies, waits for them, and re-layouts  7.6 us (11%)
    pallas_call x1, Pallas kernels, attend(): pl.pallas_call(attend_kernel, grid_spec=pltpu.PrefetchScalarGridSpec(num_...  20.6 us
    pallas_call x1, Pallas kernels, exchange(): pl.pallas_call(functools.partial(exchange_kernel, n_ctx), in_specs=[vmem,...  16.9 us
    pallas_call x1, Pallas kernels, encode(): pl.pallas_call(encode_kernel, grid_spec=pltpu.PrefetchScalarGridSpec(num_...  14.4 us
    unnamed x29, local copies, waits for them, and re-layouts  7.39 us
    pallas_call x1, Pallas kernels, build_table(): pl.pallas_call(functools.partial(table_kernel, n_space, n_ctx), in_specs=...  6.74 us

profile of v3, /device:TPU:16, one launch (start us, length us, event | category | flops | bytes accessed | tf_op | source)
XLA Modules:
  0.0 66.4 jit_solution(11735232264052050500)
XLA Ops:
  0.0 0.7 %copy-done.13 = s32[1,256]{1,0:T(1,128)S(1)} copy-done((s32[1,256]{1,0:T(1,128)S(1)}, s32[1,256]{1,0:T(1,128)}, u32[]{:S(2)}) %copy-start.13) | copy-done | bytes 1048
  0.7 0.1 copy.16.rows_ref
  0.8 0.0 copy-start.4
  0.8 1.0 %copy-done.4 = bf16[1,1024,256]{2,1,0:T(8,128)(2,1)S(1)} copy-done((bf16[1,1024,256]{2,1,0:T(8,128)(2,1)S(1)}, bf16[1,1024,256]{2,1,0:T(8,128)(2,1)}, u32[]{:S(2)}) %copy-start.4) | copy-done | bytes 524312
  1.9 6.7 %shard_map.118.table_ref = bf16[2048,256]{1,0:T(8,128)(2,1)S(1)} custom-call(s32[256,1]{1,0:T(8,128)S(1)} %copy.16.rows_ref, bf16[1024,256]{1,0:T(8,128)(2,1)S(1)} %bitcast.11), custom_call_target="tpu_custom_call" | custom-call | tf_op jit(solution)/shard_map/pallas_call | solution.py:78
  8.6 0.0 copy-done.11
  8.6 0.0 copy-start
  8.6 0.0 copy-start.8
  8.7 0.0 copy-start.9
  8.7 0.2 copy.15
  8.9 0.0 copy-start.6
  8.9 0.0 copy-start.7
  8.9 0.7 %copy-done = bf16[256,768]{1,0:T(8,128)(2,1)S(1)} copy-done((bf16[256,768]{1,0:T(8,128)(2,1)S(1)}, bf16[256,768]{1,0:T(8,128)(2,1)}, u32[]{:S(2)}) %copy-start) | copy-done | bytes 393240
  9.6 0.0 copy-start.3
  9.7 1.2 %copy-done.3 = bf16[7,256,256]{2,1,0:T(8,128)(2,1)S(1)} copy-done((bf16[7,256,256]{2,1,0:T(8,128)(2,1)S(1)}, bf16[7,256,256]{2,1,0:T(8,128)(2,1)}, u32[]{:S(2)}) %copy-start.3) | copy-done | bytes 917528
  10.8 14.4 %shard_map.119 = (f32[1024,256]{1,0:T(8,128)S(1)}, bf16[1024,256]{1,0:T(8,128)(2,1)S(1)}, bf16[1024,512]{1,0:T(8,128)(2,1)S(1)}, bf16[8,128,256]{2,1,0:T(8,128)(2,1)S(1)}, bf16[2,128,256]{2,1,0:T(8,128)(2,1)S(1)}) custom-call(s32[8,8]{1,0:T(8,128)S(1)} %bitcast.12, s32[1024,6]{1,0:T(8,128)S(1)} %bitcast.10, bf16[2048,256]{1,0:T(8,128)(2,1)S(1)} %shard_map.118.table_ref, ...), custom_call_target="tpu_custom_call" | custom-call | tf_op jit(solution)/shard_map/pallas_call | solution.py:217
  25.2 1.0 %copy-done.1 = bf16[1024,512]{1,0:T(8,128)(2,1)} copy-done((bf16[1024,512]{1,0:T(8,128)(2,1)}, bf16[1024,512]{1,0:T(8,128)(2,1)S(1)}, u32[]{:S(2)}) %copy-start.1) | copy-done | bytes 1048600
  26.2 16.9 %shard_map.120.far_ref = bf16[10,128,256]{2,1,0:T(8,128)(2,1)S(1)} custom-call(bf16[8,128,256]{2,1,0:T(8,128)(2,1)S(1)} %get-tuple-element.12.out_ref, bf16[2,128,256]{2,1,0:T(8,128)(2,1)S(1)} %get-tuple-element.13.ends_ref), custom_call_target="tpu_custom_call" | custom-call | tf_op jit(solution)/shard_map/pallas_call | solution.py:150
  43.1 0.0 copy-start.12
  43.2 0.7 %copy-done.12 = s32[1,8,4]{1,2,0:T(4,128)S(1)} copy-done((s32[1,8,4]{1,2,0:T(4,128)S(1)}, s32[1,8,4]{1,2,0:T(4,128)}, u32[]{:S(2)}) %copy-start.12) | copy-done | bytes 152
  43.8 0.1 copy.17.slots_ref
  43.9 0.7 copy-done.10
  44.6 1.2 %copy-done.2 = bf16[1024,512]{1,0:T(8,128)(2,1)S(1)} copy-done((bf16[1024,512]{1,0:T(8,128)(2,1)S(1)}, bf16[1024,512]{1,0:T(8,128)(2,1)}, u32[]{:S(2)}) %copy-start.2) | copy-done | bytes 1048600
  45.8 20.6 %shard_map.121 = bf16[1024,256]{1,0:T(8,128)(2,1)} custom-call(s32[8,4]{1,0:T(8,128)S(1)} %copy.17.slots_ref, s32[64]{0:T(128)S(1)} %bitcast.17, s32[8,8]{1,0:T(8,128)S(1)} %bitcast.13, bf16[1024,256]{1,0:T(8,128)(2,1)S(1)} %get-tuple-element.10.query_ref, bf16[1024,512]{1,0:T(8,128)(2,1)S(1)} %copy-done.2, bf16[10,128,256]{2,1,0:T(8,128)(2,1)S(1)} %shard_map.120.far_ref, ...), custom_call_target="tpu_custom_call" | custom-call | tf_op jit(solution)/shard_map/pallas_call | solution.py:328
  (11 shorter events, 0.0 us)
Async XLA Ops:
  0.0 0.7 %copy-start.13 = (s32[1,256]{1,0:T(1,128)S(1)}, s32[1,256]{1,0:T(1,128)}, u32[]{:S(2)}) copy-start(s32[1,256]{1,0:T(1,128)} %param.13) | copy-start | bytes 3076
  0.8 1.0 %copy-start.4 = (bf16[1,1024,256]{2,1,0:T(8,128)(2,1)S(1)}, bf16[1,1024,256]{2,1,0:T(8,128)(2,1)}, u32[]{:S(2)}) copy-start(bf16[1,1024,256]{2,1,0:T(8,128)(2,1)} %param.12) | copy-start | bytes 1572868
  1.9 6.8 %copy-start.11 = (s32[1,1024,6]{1,0,2:T(1,128)S(1)}, s32[1,1024,6]{1,0,2:T(1,128)}, u32[]{:S(2)}) copy-start(s32[1,1024,6]{1,0,2:T(1,128)} %param.14) | copy-start | bytes 73732
  8.6 1.0 %copy-start = (bf16[256,768]{1,0:T(8,128)(2,1)S(1)}, bf16[256,768]{1,0:T(8,128)(2,1)}, u32[]{:S(2)}) copy-start(bf16[256,768]{1,0:T(8,128)(2,1)} %qkv_ref.3) | copy-start | bytes 1179652
  8.6 1.0 %copy-start.8 = (f32[256]{0:T(256)S(1)}, f32[256]{0:T(256)}, u32[]{:S(2)}) copy-start(f32[256]{0:T(256)} %param.20) | copy-start | bytes 3076
  8.7 1.0 %copy-start.9 = (f32[256]{0:T(256)S(1)}, f32[256]{0:T(256)}, u32[]{:S(2)}) copy-start(f32[256]{0:T(256)} %param.21) | copy-start | bytes 3076
  8.9 0.7 %copy-start.6 = (s32[1,8,8]{2,1,0:T(8,128)S(1)}, s32[1,8,8]{2,1,0:T(8,128)}, u32[]{:S(2)}) copy-start(s32[1,8,8]{2,1,0:T(8,128)} %param.17) | copy-start | bytes 772
  8.9 0.7 %copy-start.7 = (f32[256]{0:T(256)S(1)}, f32[256]{0:T(256)}, u32[]{:S(2)}) copy-start(f32[256]{0:T(256)} %param.19) | copy-start | bytes 3076
  9.6 1.2 %copy-start.3 = (bf16[7,256,256]{2,1,0:T(8,128)(2,1)S(1)}, bf16[7,256,256]{2,1,0:T(8,128)(2,1)}, u32[]{:S(2)}) copy-start(bf16[7,256,256]{2,1,0:T(8,128)(2,1)} %weight_ref.1) | copy-start | bytes 2752516
  25.2 1.0 %copy-start.1 = (bf16[1024,512]{1,0:T(8,128)(2,1)}, bf16[1024,512]{1,0:T(8,128)(2,1)S(1)}, u32[]{:S(2)}) copy-start(bf16[1024,512]{1,0:T(8,128)(2,1)S(1)} %get-tuple-element.11.near_ref) | copy-start | bytes 3145732
  26.2 17.7 %copy-start.5 = (bf16[256,256]{1,0:T(8,128)(2,1)S(1)}, bf16[256,256]{1,0:T(8,128)(2,1)}, u32[]{:S(2)}) copy-start(bf16[256,256]{1,0:T(8,128)(2,1)} %out_w_ref.1) | copy-start | bytes 393220
  43.1 0.7 %copy-start.12 = (s32[1,8,4]{1,2,0:T(4,128)S(1)}, s32[1,8,4]{1,2,0:T(4,128)}, u32[]{:S(2)}) copy-start(s32[1,8,4]{1,2,0:T(4,128)} %param.16) | copy-start | bytes 388
  43.9 0.7 copy-start.10
  44.6 1.2 %copy-start.2 = (bf16[1024,512]{1,0:T(8,128)(2,1)S(1)}, bf16[1024,512]{1,0:T(8,128)(2,1)}, u32[]{:S(2)}) copy-start(bf16[1024,512]{1,0:T(8,128)(2,1)} %copy-done.1) | copy-start | bytes 3145732

commit v4 on v3

--- a/solution.py
+++ b/solution.py
@@ -163,7 +163,7 @@
     )(outgoing, ends)
 
 
-ROWS = 256
+ROWS = 1024
 
 
 def encode_kernel(
@@ -241,6 +241,8 @@
 
 
 HALF = 128
+CHUNK = 4
+AHEAD = 1
 
 
 def attend_kernel(
@@ -293,27 +295,35 @@
     heads = HALF // head_dim
     adds_mask = jnp.where(lane == 0, 1.0, 0.0).astype(jnp.bfloat16)
     scale = math.log2(math.e) / math.sqrt(head_dim)
-    halves = []
-    for group in range(D // HALF):
+    chunks = [(group, first) for group in range(D // HALF) for first in range(0, heads, CHUNK)]
+
+    def score(group, first):
         query = query_ref[:, group * HALF : (group + 1) * HALF]
         stacked = jnp.concatenate(
             [
                 jnp.concatenate([jnp.where(head_of == head, query, jnp.zeros_like(query)), adds_mask], 1)
-                for head in range(heads)
+                for head in range(first, first + CHUNK)
             ],
             0,
         )
-        scores = lax.dot_general(
+        return lax.dot_general(
             stacked, keys_ref[group], (((1,), (1,)), ((), ())), preferred_element_type=jnp.float32
         )
+
+    halves = [jnp.zeros((BLK, HALF), jnp.float32) for _ in range(D // HALF)]
+    ahead = [score(*chunk) for chunk in chunks[:AHEAD]]
+    for turn, (group, first) in enumerate(chunks):
+        if turn + AHEAD < len(chunks):
+            ahead.append(score(*chunks[turn + AHEAD]))
+        scores = ahead[turn]
         peak = jnp.max(scores, axis=-1, keepdims=True)
         weights = jnp.exp2((scores - peak) * scale).astype(jnp.bfloat16)
         mixed = jnp.dot(weights, values_ref[group], preferred_element_type=jnp.float32)
         mixed = mixed[:, :HALF] / mixed[:, HALF:]
-        half = mixed[:BLK]
-        for head in range(1, heads):
-            half = jnp.where(head_of == head, mixed[head * BLK : (head + 1) * BLK], half)
-        halves.append(half)
+        for head in range(CHUNK):
+            halves[group] = jnp.where(
+                head_of == first + head, mixed[head * BLK : (head + 1) * BLK], halves[group]
+            )
     attended = jnp.concatenate(halves, 1)
     out = hidden_ref[...] + jnp.dot(
         attended.astype(jnp.bfloat16), out_w_ref[...], preferred_element_type=jnp.float32

time: 66.7 us -> 60.1 us (0.901)
  Pallas kernels: 58.7 us -> 52 us
    pallas_call x1, Pallas kernels: 20.6 us -> 16.4 us  [attend(): pl.pallas_call(attend_kernel, grid_spec=pltpu.PrefetchScalarGridSpec(num_...]
    pallas_call x1, Pallas kernels: 14.4 us -> 12 us  [encode(): pl.pallas_call(encode_kernel, grid_spec=pltpu.PrefetchScalarGridSpec(num_...]
where the time goes in v4:
time: 60.1 us; the launch traced here: 59.8 us
  Pallas kernels  52 us (87%)
  local copies, waits for them, and re-layouts  7.6 us (13%)
    pallas_call x1, Pallas kernels, exchange(): pl.pallas_call(functools.partial(exchange_kernel, n_ctx), in_specs=[vmem,...  16.9 us
    pallas_call x1, Pallas kernels, attend(): pl.pallas_call(attend_kernel, grid_spec=pltpu.PrefetchScalarGridSpec(num_...  16.4 us
    pallas_call x1, Pallas kernels, encode(): pl.pallas_call(encode_kernel, grid_spec=pltpu.PrefetchScalarGridSpec(num_...  12 us
    unnamed x29, local copies, waits for them, and re-layouts  7.39 us
    pallas_call x1, Pallas kernels, build_table(): pl.pallas_call(functools.partial(table_kernel, n_space, n_ctx), in_specs=...  6.74 us

profile of v4, /device:TPU:16, one launch (start us, length us, event | category | flops | bytes accessed | tf_op | source)
XLA Modules:
  0.0 59.8 jit_solution(8019312880828927049)
XLA Ops:
  0.0 0.7 %copy-done.13 = s32[1,256]{1,0:T(1,128)S(1)} copy-done((s32[1,256]{1,0:T(1,128)S(1)}, s32[1,256]{1,0:T(1,128)}, u32[]{:S(2)}) %copy-start.13) | copy-done | bytes 1048
  0.7 0.1 copy.16.rows_ref
  0.8 0.0 copy-start.4
  0.8 1.0 %copy-done.4 = bf16[1,1024,256]{2,1,0:T(8,128)(2,1)S(1)} copy-done((bf16[1,1024,256]{2,1,0:T(8,128)(2,1)S(1)}, bf16[1,1024,256]{2,1,0:T(8,128)(2,1)}, u32[]{:S(2)}) %copy-start.4) | copy-done | bytes 524312
  1.9 6.7 %shard_map.118.table_ref = bf16[2048,256]{1,0:T(8,128)(2,1)S(1)} custom-call(s32[256,1]{1,0:T(8,128)S(1)} %copy.16.rows_ref, bf16[1024,256]{1,0:T(8,128)(2,1)S(1)} %bitcast.11), custom_call_target="tpu_custom_call" | custom-call | tf_op jit(solution)/shard_map/pallas_call | solution.py:78
  8.6 0.0 copy-done.11
  8.6 0.0 copy-start
  8.6 0.0 copy-start.8
  8.7 0.0 copy-start.9
  8.7 0.2 copy.15
  8.9 0.0 copy-start.6
  8.9 0.0 copy-start.7
  8.9 0.7 %copy-done = bf16[256,768]{1,0:T(8,128)(2,1)S(1)} copy-done((bf16[256,768]{1,0:T(8,128)(2,1)S(1)}, bf16[256,768]{1,0:T(8,128)(2,1)}, u32[]{:S(2)}) %copy-start) | copy-done | bytes 393240
  9.6 0.0 copy-start.3
  9.7 1.2 %copy-done.3 = bf16[7,256,256]{2,1,0:T(8,128)(2,1)S(1)} copy-done((bf16[7,256,256]{2,1,0:T(8,128)(2,1)S(1)}, bf16[7,256,256]{2,1,0:T(8,128)(2,1)}, u32[]{:S(2)}) %copy-start.3) | copy-done | bytes 917528
  10.8 12.0 %shard_map.119 = (f32[1024,256]{1,0:T(8,128)S(1)}, bf16[1024,256]{1,0:T(8,128)(2,1)S(1)}, bf16[1024,512]{1,0:T(8,128)(2,1)S(1)}, bf16[8,128,256]{2,1,0:T(8,128)(2,1)S(1)}, bf16[2,128,256]{2,1,0:T(8,128)(2,1)S(1)}) custom-call(s32[8,8]{1,0:T(8,128)S(1)} %bitcast.12, s32[1024,6]{1,0:T(8,128)S(1)} %bitcast.10, bf16[2048,256]{1,0:T(8,128)(2,1)S(1)} %shard_map.118.table_ref, ...), custom_call_target="tpu_custom_call" | custom-call | tf_op jit(solution)/shard_map/pallas_call | solution.py:217
  22.8 1.0 %copy-done.1 = bf16[1024,512]{1,0:T(8,128)(2,1)} copy-done((bf16[1024,512]{1,0:T(8,128)(2,1)}, bf16[1024,512]{1,0:T(8,128)(2,1)S(1)}, u32[]{:S(2)}) %copy-start.1) | copy-done | bytes 1048600
  23.8 16.9 %shard_map.120.far_ref = bf16[10,128,256]{2,1,0:T(8,128)(2,1)S(1)} custom-call(bf16[8,128,256]{2,1,0:T(8,128)(2,1)S(1)} %get-tuple-element.12.out_ref, bf16[2,128,256]{2,1,0:T(8,128)(2,1)S(1)} %get-tuple-element.13.ends_ref), custom_call_target="tpu_custom_call" | custom-call | tf_op jit(solution)/shard_map/pallas_call | solution.py:150
  40.7 0.0 copy-start.12
  40.7 0.7 %copy-done.12 = s32[1,8,4]{1,2,0:T(4,128)S(1)} copy-done((s32[1,8,4]{1,2,0:T(4,128)S(1)}, s32[1,8,4]{1,2,0:T(4,128)}, u32[]{:S(2)}) %copy-start.12) | copy-done | bytes 152
  41.4 0.1 copy.17.slots_ref
  41.5 0.7 %copy-done.10 = s32[1,64]{1,0:T(1,128)S(1)} copy-done((s32[1,64]{1,0:T(1,128)S(1)}, s32[1,64]{1,0:T(1,128)}, u32[]{:S(2)}) %copy-start.10) | copy-done | bytes 280
  42.1 1.2 %copy-done.2 = bf16[1024,512]{1,0:T(8,128)(2,1)S(1)} copy-done((bf16[1024,512]{1,0:T(8,128)(2,1)S(1)}, bf16[1024,512]{1,0:T(8,128)(2,1)}, u32[]{:S(2)}) %copy-start.2) | copy-done | bytes 1048600
  43.4 16.4 %shard_map.121 = bf16[1024,256]{1,0:T(8,128)(2,1)} custom-call(s32[8,4]{1,0:T(8,128)S(1)} %copy.17.slots_ref, s32[64]{0:T(128)S(1)} %bitcast.17, s32[8,8]{1,0:T(8,128)S(1)} %bitcast.13, bf16[1024,256]{1,0:T(8,128)(2,1)S(1)} %get-tuple-element.10.query_ref, bf16[1024,512]{1,0:T(8,128)(2,1)S(1)} %copy-done.2, bf16[10,128,256]{2,1,0:T(8,128)(2,1)S(1)} %shard_map.120.far_ref, ...), custom_call_target="tpu_custom_call" | custom-call | tf_op jit(solution)/shard_map/pallas_call | solution.py:338
  (11 shorter events, 0.0 us)
Async XLA Ops:
  0.0 0.7 %copy-start.13 = (s32[1,256]{1,0:T(1,128)S(1)}, s32[1,256]{1,0:T(1,128)}, u32[]{:S(2)}) copy-start(s32[1,256]{1,0:T(1,128)} %param.13) | copy-start | bytes 3076
  0.8 1.0 %copy-start.4 = (bf16[1,1024,256]{2,1,0:T(8,128)(2,1)S(1)}, bf16[1,1024,256]{2,1,0:T(8,128)(2,1)}, u32[]{:S(2)}) copy-start(bf16[1,1024,256]{2,1,0:T(8,128)(2,1)} %param.12) | copy-start | bytes 1572868
  1.9 6.8 %copy-start.11 = (s32[1,1024,6]{1,0,2:T(1,128)S(1)}, s32[1,1024,6]{1,0,2:T(1,128)}, u32[]{:S(2)}) copy-start(s32[1,1024,6]{1,0,2:T(1,128)} %param.14) | copy-start | bytes 73732
  8.6 1.0 %copy-start = (bf16[256,768]{1,0:T(8,128)(2,1)S(1)}, bf16[256,768]{1,0:T(8,128)(2,1)}, u32[]{:S(2)}) copy-start(bf16[256,768]{1,0:T(8,128)(2,1)} %qkv_ref.3) | copy-start | bytes 1179652
  8.6 1.0 %copy-start.8 = (f32[256]{0:T(256)S(1)}, f32[256]{0:T(256)}, u32[]{:S(2)}) copy-start(f32[256]{0:T(256)} %param.20) | copy-start | bytes 3076
  8.7 1.0 %copy-start.9 = (f32[256]{0:T(256)S(1)}, f32[256]{0:T(256)}, u32[]{:S(2)}) copy-start(f32[256]{0:T(256)} %param.21) | copy-start | bytes 3076
  8.9 0.7 %copy-start.6 = (s32[1,8,8]{2,1,0:T(8,128)S(1)}, s32[1,8,8]{2,1,0:T(8,128)}, u32[]{:S(2)}) copy-start(s32[1,8,8]{2,1,0:T(8,128)} %param.17) | copy-start | bytes 772
  8.9 0.7 %copy-start.7 = (f32[256]{0:T(256)S(1)}, f32[256]{0:T(256)}, u32[]{:S(2)}) copy-start(f32[256]{0:T(256)} %param.19) | copy-start | bytes 3076
  9.6 1.2 %copy-start.3 = (bf16[7,256,256]{2,1,0:T(8,128)(2,1)S(1)}, bf16[7,256,256]{2,1,0:T(8,128)(2,1)}, u32[]{:S(2)}) copy-start(bf16[7,256,256]{2,1,0:T(8,128)(2,1)} %weight_ref.1) | copy-start | bytes 2752516
  22.8 1.0 %copy-start.1 = (bf16[1024,512]{1,0:T(8,128)(2,1)}, bf16[1024,512]{1,0:T(8,128)(2,1)S(1)}, u32[]{:S(2)}) copy-start(bf16[1024,512]{1,0:T(8,128)(2,1)S(1)} %get-tuple-element.11.near_ref) | copy-start | bytes 3145732
  23.8 17.7 %copy-start.5 = (bf16[256,256]{1,0:T(8,128)(2,1)S(1)}, bf16[256,256]{1,0:T(8,128)(2,1)}, u32[]{:S(2)}) copy-start(bf16[256,256]{1,0:T(8,128)(2,1)} %out_w_ref.1) | copy-start | bytes 393220
  40.7 0.7 %copy-start.12 = (s32[1,8,4]{1,2,0:T(4,128)S(1)}, s32[1,8,4]{1,2,0:T(4,128)}, u32[]{:S(2)}) copy-start(s32[1,8,4]{1,2,0:T(4,128)} %param.16) | copy-start | bytes 388
  41.5 0.7 %copy-start.10 = (s32[1,64]{1,0:T(1,128)S(1)}, s32[1,64]{1,0:T(1,128)}, u32[]{:S(2)}) copy-start(s32[1,64]{1,0:T(1,128)} %param.15) | copy-start | bytes 772
  42.1 1.2 %copy-start.2 = (bf16[1024,512]{1,0:T(8,128)(2,1)S(1)}, bf16[1024,512]{1,0:T(8,128)(2,1)}, u32[]{:S(2)}) copy-start(bf16[1024,512]{1,0:T(8,128)(2,1)} %copy-done.1) | copy-start | bytes 3145732

commit v5 on v4

--- a/solution.py
+++ b/solution.py
@@ -230,7 +230,7 @@
             scratch_shapes=[pltpu.VMEM((count, width), jnp.bfloat16)],
         ),
         out_shape=[
-            jax.ShapeDtypeStruct((count, width), jnp.float32),
+            pltpu.HBM((count, width), jnp.float32),
             jax.ShapeDtypeStruct((count, width), jnp.bfloat16),
             jax.ShapeDtypeStruct((count, 2 * width), jnp.bfloat16),
             jax.ShapeDtypeStruct((peers, BLK, width), jnp.bfloat16),
@@ -376,6 +376,7 @@
     hidden, queries, near, outgoing, ends = encode(
         pick[0], neighbours[0], table, cpe_weight, cpe_bias, ln_gain, ln_bias, w_qkv
     )
+    hidden = pltpu.with_memory_space_constraint(hidden, pltpu.HBM)
     far = exchange(outgoing, ends, n_ctx)
     return attend(dilated[0], block_len[0], pick[0], queries, near, far, w_qkv, hidden, w_out)[None]
 

time: 60.1 us -> 59.1 us (0.983)
  local copies, waits for them, and re-layouts: 7.6 us -> 5.4 us
  Pallas kernels: 52 us -> 53.3 us
    unnamed x29 -> x25, local copies, waits for them, and re-layouts: 7.39 us -> 5.19 us
    pallas_call x1, Pallas kernels: 16.4 us -> 17.3 us  [attend(): pl.pallas_call(attend_kernel, grid_spec=pltpu.PrefetchScalarGridSpec(num_...]
where the time goes in v5:
time: 59.1 us; the launch traced here: 58.8 us
  Pallas kernels  53.3 us (90%)
  local copies, waits for them, and re-layouts  5.4 us (9%)
    pallas_call x1, Pallas kernels, attend(): pl.pallas_call(attend_kernel, grid_spec=pltpu.PrefetchScalarGridSpec(num_...  17.3 us
    pallas_call x1, Pallas kernels, exchange(): pl.pallas_call(functools.partial(exchange_kernel, n_ctx), in_specs=[vmem,...  16.9 us
    pallas_call x1, Pallas kernels, encode(): pl.pallas_call(encode_kernel, grid_spec=pltpu.PrefetchScalarGridSpec(num_...  12.3 us
    pallas_call x1, Pallas kernels, build_table(): pl.pallas_call(functools.partial(table_kernel, n_space, n_ctx), in_specs=...  6.74 us
    unnamed x25, local copies, waits for them, and re-layouts  5.19 us

profile of v5, /device:TPU:16, one launch (start us, length us, event | category | flops | bytes accessed | tf_op | source)
XLA Modules:
  0.0 58.8 jit_solution(9347330096440421822)
XLA Ops:
  0.0 0.7 %copy-done.11 = s32[1,256]{1,0:T(1,128)S(1)} copy-done((s32[1,256]{1,0:T(1,128)S(1)}, s32[1,256]{1,0:T(1,128)}, u32[]{:S(2)}) %copy-start.11) | copy-done | bytes 1048
  0.7 0.1 copy.16.rows_ref
  0.8 0.0 copy-start.2
  0.8 1.0 %copy-done.2 = bf16[1,1024,256]{2,1,0:T(8,128)(2,1)S(1)} copy-done((bf16[1,1024,256]{2,1,0:T(8,128)(2,1)S(1)}, bf16[1,1024,256]{2,1,0:T(8,128)(2,1)}, u32[]{:S(2)}) %copy-start.2) | copy-done | bytes 524312
  1.9 6.7 %shard_map.118.table_ref = bf16[2048,256]{1,0:T(8,128)(2,1)S(1)} custom-call(s32[256,1]{1,0:T(8,128)S(1)} %copy.16.rows_ref, bf16[1024,256]{1,0:T(8,128)(2,1)S(1)} %bitcast.11), custom_call_target="tpu_custom_call" | custom-call | tf_op jit(solution)/shard_map/pallas_call | solution.py:78
  8.6 0.0 copy-done.9
  8.6 0.0 copy-start
  8.6 0.0 copy-start.6
  8.7 0.0 copy-start.7
  8.7 0.2 copy.15
  8.9 0.0 copy-start.4
  8.9 0.0 copy-start.5
  8.9 0.7 %copy-done = bf16[256,768]{1,0:T(8,128)(2,1)S(1)} copy-done((bf16[256,768]{1,0:T(8,128)(2,1)S(1)}, bf16[256,768]{1,0:T(8,128)(2,1)}, u32[]{:S(2)}) %copy-start) | copy-done | bytes 393240
  9.6 0.0 copy-done.6
  9.6 0.0 copy-done.7
  9.6 0.0 copy-start.1
  9.7 1.2 %copy-done.1 = bf16[7,256,256]{2,1,0:T(8,128)(2,1)S(1)} copy-done((bf16[7,256,256]{2,1,0:T(8,128)(2,1)S(1)}, bf16[7,256,256]{2,1,0:T(8,128)(2,1)}, u32[]{:S(2)}) %copy-start.1) | copy-done | bytes 917528
  10.8 12.3 %shard_map.119 = (f32[1024,256]{1,0:T(8,128)}, bf16[1024,256]{1,0:T(8,128)(2,1)S(1)}, bf16[1024,512]{1,0:T(8,128)(2,1)S(1)}, bf16[8,128,256]{2,1,0:T(8,128)(2,1)S(1)}, bf16[2,128,256]{2,1,0:T(8,128)(2,1)S(1)}) custom-call(s32[8,8]{1,0:T(8,128)S(1)} %bitcast.12, s32[1024,6]{1,0:T(8,128)S(1)} %bitcast.10, bf16[2048,256]{1,0:T(8,128)(2,1)S(1)} %shard_map.118.table_ref, ...), custom_call_target="tpu_custom_call" | custom-call | tf_op jit(solution)/shard_map/pallas_call | solution.py:217
  23.2 16.9 %shard_map.120.far_ref = bf16[10,128,256]{2,1,0:T(8,128)(2,1)S(1)} custom-call(bf16[8,128,256]{2,1,0:T(8,128)(2,1)S(1)} %get-tuple-element.12.out_ref, bf16[2,128,256]{2,1,0:T(8,128)(2,1)S(1)} %get-tuple-element.13.ends_ref), custom_call_target="tpu_custom_call" | custom-call | tf_op jit(solution)/shard_map/pallas_call | solution.py:150
  40.1 0.0 copy-start.10
  40.1 0.7 %copy-done.10 = s32[1,8,4]{1,2,0:T(4,128)S(1)} copy-done((s32[1,8,4]{1,2,0:T(4,128)S(1)}, s32[1,8,4]{1,2,0:T(4,128)}, u32[]{:S(2)}) %copy-start.10) | copy-done | bytes 152
  40.8 0.1 copy.17.slots_ref
  40.8 0.7 %copy-done.8 = s32[1,64]{1,0:T(1,128)S(1)} copy-done((s32[1,64]{1,0:T(1,128)S(1)}, s32[1,64]{1,0:T(1,128)}, u32[]{:S(2)}) %copy-start.8) | copy-done | bytes 280
  41.5 17.3 %shard_map.121 = bf16[1024,256]{1,0:T(8,128)(2,1)} custom-call(s32[8,4]{1,0:T(8,128)S(1)} %copy.17.slots_ref, s32[64]{0:T(128)S(1)} %bitcast.17, s32[8,8]{1,0:T(8,128)S(1)} %bitcast.13, bf16[1024,256]{1,0:T(8,128)(2,1)S(1)} %get-tuple-element.10.query_ref, bf16[1024,512]{1,0:T(8,128)(2,1)S(1)} %get-tuple-element.11.near_ref, ...), custom_call_target="tpu_custom_call" | custom-call | tf_op jit(solution)/shard_map/pallas_call | solution.py:338
  (7 shorter events, 0.0 us)
Async XLA Ops:
  0.0 0.7 %copy-start.11 = (s32[1,256]{1,0:T(1,128)S(1)}, s32[1,256]{1,0:T(1,128)}, u32[]{:S(2)}) copy-start(s32[1,256]{1,0:T(1,128)} %param.13) | copy-start | bytes 3076
  0.8 1.0 %copy-start.2 = (bf16[1,1024,256]{2,1,0:T(8,128)(2,1)S(1)}, bf16[1,1024,256]{2,1,0:T(8,128)(2,1)}, u32[]{:S(2)}) copy-start(bf16[1,1024,256]{2,1,0:T(8,128)(2,1)} %param.12) | copy-start | bytes 1572868
  1.9 6.8 %copy-start.9 = (s32[1,1024,6]{1,0,2:T(1,128)S(1)}, s32[1,1024,6]{1,0,2:T(1,128)}, u32[]{:S(2)}) copy-start(s32[1,1024,6]{1,0,2:T(1,128)} %param.14) | copy-start | bytes 73732
  8.6 1.0 %copy-start = (bf16[256,768]{1,0:T(8,128)(2,1)S(1)}, bf16[256,768]{1,0:T(8,128)(2,1)}, u32[]{:S(2)}) copy-start(bf16[256,768]{1,0:T(8,128)(2,1)} %qkv_ref.3) | copy-start | bytes 1179652
  8.6 1.0 %copy-start.6 = (f32[256]{0:T(256)S(1)}, f32[256]{0:T(256)}, u32[]{:S(2)}) copy-start(f32[256]{0:T(256)} %param.20) | copy-start | bytes 3076
  8.7 1.0 %copy-start.7 = (f32[256]{0:T(256)S(1)}, f32[256]{0:T(256)}, u32[]{:S(2)}) copy-start(f32[256]{0:T(256)} %param.21) | copy-start | bytes 3076
  8.9 0.7 %copy-start.4 = (s32[1,8,8]{2,1,0:T(8,128)S(1)}, s32[1,8,8]{2,1,0:T(8,128)}, u32[]{:S(2)}) copy-start(s32[1,8,8]{2,1,0:T(8,128)} %param.17) | copy-start | bytes 772
  8.9 0.7 %copy-start.5 = (f32[256]{0:T(256)S(1)}, f32[256]{0:T(256)}, u32[]{:S(2)}) copy-start(f32[256]{0:T(256)} %param.19) | copy-start | bytes 3076
  9.6 1.2 %copy-start.1 = (bf16[7,256,256]{2,1,0:T(8,128)(2,1)S(1)}, bf16[7,256,256]{2,1,0:T(8,128)(2,1)}, u32[]{:S(2)}) copy-start(bf16[7,256,256]{2,1,0:T(8,128)(2,1)} %weight_ref.1) | copy-start | bytes 2752516
  23.2 17.7 %copy-start.3 = (bf16[256,256]{1,0:T(8,128)(2,1)S(1)}, bf16[256,256]{1,0:T(8,128)(2,1)}, u32[]{:S(2)}) copy-start(bf16[256,256]{1,0:T(8,128)(2,1)} %out_w_ref.1) | copy-start | bytes 393220
  40.1 0.7 %copy-start.10 = (s32[1,8,4]{1,2,0:T(4,128)S(1)}, s32[1,8,4]{1,2,0:T(4,128)}, u32[]{:S(2)}) copy-start(s32[1,8,4]{1,2,0:T(4,128)} %param.16) | copy-start | bytes 388
  40.8 0.7 %copy-start.8 = (s32[1,64]{1,0:T(1,128)S(1)}, s32[1,64]{1,0:T(1,128)}, u32[]{:S(2)}) copy-start(s32[1,64]{1,0:T(1,128)} %param.15) | copy-start | bytes 772
